TPU v7x, 32 devices: a whole 2x2x4 slice. The times are simulated.
32 devices in a mesh: pipe: 4 (over y, x), seq: 8 (over z, core).
Axes of the slice: x: 2, y: 2, z: 4, core: 2. Of those that a mesh axis runs over, the one named last changes fastest.
Arguments:
- latents: bfloat16 [2, 64, 1536], P(None, 'seq', 'pipe'), may hold values from -6 to 6
- timesteps: int32 [2, 2], replicated, may hold values from 0 to 15
- step_sizes: float32 [16], replicated, may hold values from 0.2 to 0.8
- mod_table: float32 [4, 16, 4608], P('pipe'), may hold values from -4 to 4
- qk_gain: float32 [4, 2, 128], P('pipe'), may hold values from 0.5 to 2
- w_query: bfloat16 [4, 1536, 1536], P('pipe'), may hold values from -0.15625 to 0.15625
- w_kv: bfloat16 [4, 1536, 3072], P('pipe', 'seq'), may hold values from -0.15625 to 0.15625
- w_out: bfloat16 [4, 1536, 1536], P('pipe'), may hold values from -0.15625 to 0.15625
Outputs:
- final_latents: bfloat16 [2, 64, 1536], P(None, 'seq', 'pipe')
All inputs are finite; a program needn't handle non-finite values.
Results may differ from a plain program's by a relative error of at most 0.025.
Values may be sent and summed in bfloat16 or wider, within the bound.
A program may use at most 64 MiB of HBM per device.

v0:
```python
import math

import jax
import jax.numpy as jnp
from jax import lax
from jax.sharding import PartitionSpec as P

norm_eps = 1e-06


def passed_along(value, axis, steps):
    count = lax.axis_size(axis)
    pairs = [(source, (source + steps) % count) for source in range(count)]
    return lax.ppermute(value, axis, pairs)


def from_root(value, axis, source):
    kept = jnp.where(lax.axis_index(axis) == source, value, 0).astype(value.dtype)
    return lax.psum(kept, axis)


def rms_heads(values, gain_row):
    mean_square = jnp.mean(values * values, axis=-1, keepdims=True)
    return values * lax.rsqrt(mean_square + norm_eps) * gain_row


def modulate(hidden, shift_row, scale_row):
    as_float = hidden.astype(jnp.float32)
    center = jnp.mean(as_float, axis=-1, keepdims=True)
    spread = jnp.mean(jnp.square(as_float - center), axis=-1, keepdims=True)
    return (
        (as_float - center) * lax.rsqrt(spread + norm_eps) * (1.0 + scale_row) + shift_row
    ).astype(jnp.bfloat16)


def attend(queries, key_rows, value_rows, score_scale):
    logits = (
        jnp.einsum("qhd,khd->hqk", queries, key_rows, preferred_element_type=jnp.float32)
        * score_scale
    )
    weights_soft = jnp.exp(logits)
    running_sum = jnp.sum(weights_soft, axis=-1)
    weighted = jnp.einsum(
        "hqk,khd->hqd",
        weights_soft.astype(jnp.bfloat16),
        value_rows,
        preferred_element_type=jnp.float32,
    )
    return (running_sum, weighted)


def shards(latents, timesteps, step_sizes, mod_table, qk_gain, w_query, w_kv, w_out):
    n_pipe = lax.axis_size("pipe")
    segment_now = lax.axis_index("pipe")
    micro_count = latents.shape[0]
    row_count = latents.shape[1]
    feature_share = latents.shape[2]
    model_width = feature_share * n_pipe
    table_size = step_sizes.shape[0]
    inner_width = w_out.shape[1]
    head_dim = qk_gain.shape[2]
    head_count = inner_width // head_dim
    step_count = timesteps.shape[0]
    score_scale = 1.0 / math.sqrt(head_dim)
    slots = lax.all_gather(latents, "pipe", axis=2, tiled=True)
    kv_weight = lax.all_gather(w_kv, "seq", axis=1, tiled=True)[0]
    query_weight = w_query[0]
    out_weight = w_out[0]
    mod_rows = mod_table[0]
    gain_query = qk_gain[0, 0]
    gain_key = qk_gain[0, 1]

    def key_value(modded):
        projected = jnp.dot(modded, kv_weight, preferred_element_type=jnp.float32)
        projected = projected.reshape(modded.shape[0], 2, head_count, head_dim)
        key_rows = rms_heads(projected[:, 0], gain_key).astype(jnp.bfloat16)
        value_rows = projected[:, 1].astype(jnp.bfloat16)
        return (key_rows, value_rows)

    def apply_layer(hidden, time_index):
        one_hot = (jnp.arange(table_size, dtype=jnp.int32) == time_index).astype(jnp.float32)
        modulation = jnp.dot(one_hot, mod_rows, precision=lax.Precision.HIGHEST)
        shift_row = modulation[:model_width]
        scale_row = modulation[model_width : 2 * model_width]
        gate_row = modulation[2 * model_width :]
        modded = modulate(hidden, shift_row, scale_row)
        queries = jnp.dot(modded, query_weight, preferred_element_type=jnp.float32)
        queries = rms_heads(queries.reshape(row_count, head_count, head_dim), gain_query).astype(
            jnp.bfloat16
        )
        key_rows, value_rows = key_value(modded)
        running_sum, weighted = attend(
            queries,
            lax.all_gather(key_rows, "seq", axis=0, tiled=True),
            lax.all_gather(value_rows, "seq", axis=0, tiled=True),
            score_scale,
        )
        attended = (weighted / running_sum[..., None]).astype(jnp.bfloat16)
        attended = jnp.transpose(attended, (1, 0, 2)).reshape(row_count, inner_width)
        projected_out = jnp.dot(attended, out_weight, preferred_element_type=jnp.float32)
        return (hidden.astype(jnp.float32) + gate_row * projected_out).astype(jnp.bfloat16)

    def advance(tick_now, running):
        moving, latent_state = running
        offset = tick_now - segment_now
        step_now = jnp.floor_divide(offset, n_pipe)
        slot_now = jnp.mod(offset, n_pipe)
        is_live = (offset >= 0) & (slot_now < micro_count) & (step_now < step_count)
        slot_safe = jnp.clip(slot_now, 0, micro_count - 1)
        step_safe = jnp.clip(step_now, 0, step_count - 1)
        time_index = timesteps[step_safe, slot_safe]
        first_pass = (segment_now == 0) & (step_safe == 0)
        incoming = jnp.where(first_pass, slots[slot_safe], moving)
        layer_out = apply_layer(incoming, time_index)
        is_last = segment_now == n_pipe - 1
        one_hot = (jnp.arange(table_size, dtype=jnp.int32) == time_index).astype(jnp.float32)
        step_size = jnp.dot(one_hot, step_sizes, precision=lax.Precision.HIGHEST)
        previous = latent_state[slot_safe]
        update = (previous.astype(jnp.float32) - step_size * layer_out.astype(jnp.float32)).astype(
            jnp.bfloat16
        )
        new_state = jnp.where(
            is_last & is_live, latent_state.at[slot_safe].set(update), latent_state
        )
        outgoing = jnp.where(is_live, jnp.where(is_last, update, layer_out), incoming)
        moving = passed_along(outgoing, "pipe", 1)
        return (moving, new_state)

    tick_count = step_count * n_pipe + micro_count - 1
    moving = jnp.zeros((row_count, model_width), jnp.bfloat16)
    moving, latent_state = lax.fori_loop(0, tick_count, advance, (moving, slots))
    result_all = from_root(latent_state, "pipe", n_pipe - 1)
    return lax.dynamic_slice_in_dim(result_all, segment_now * feature_share, feature_share, 2)


def solution(mesh):
    in_specs = (
        P(None, "seq", "pipe"),
        P(),
        P(),
        P("pipe", None, None),
        P("pipe", None, None),
        P("pipe", None, None),
        P("pipe", "seq", None),
        P("pipe", None, None),
    )
    out_specs = P(None, "seq", "pipe")
    return jax.shard_map(shards, mesh=mesh, in_specs=in_specs, out_specs=out_specs, check_vma=False)
```

profile of v0, /device:TPU:0, one launch (start us, length us, event | category | flops | bytes accessed | tf_op | source)
XLA Modules:
  0.0 556.8 jit_solution(3101024376465565159)
XLA Ops:
  7.3 9.8 %all_gather.26 = bf16[2,8,1536]{2,1,0:T(8,128)(2,1)S(1)} all-gather(bf16[2,8,384]{2,1,0:T(8,128)(2,1)} %param.12), channel_id=1, replica_groups=mesh['pipe'=4,'seq'=8] {'pipe'}, dimensions={2}, use_global_device_ids=true | all-gather | bytes 61440 | tf_op jit(solution)/shard_map/all_gather | solution.py:65
  17.9 84.6 %all-gather.5.cloned.1.call-done = bf16[1,1536,3072]{2,1,0:T(8,128)(2,1)} async-done(((bf16[1,192,3072]{2,1,0:T(8,128)(2,1)}), bf16[1,1536,3072]{2,1,0:T(8,128)(2,1)}) %all-gather.5.cloned.1.call-update) | async-done | bytes 9437200 | tf_op jit(solution)/shard_map/all_gather | solution.py:66
  102.5 432.2 %while.18 = (s32[]{:T(128)}, bf16[8,1536]{1,0:T(8,128)(2,1)S(1)}, bf16[2,8,1536]{2,1,0:T(8,128)(2,1)S(1)}, s32[]{:T(128)}, pred[]{:T(512)}, /*index=5*/s32[2,2]{...) while((s32[]{:T(128)}, bf16[8,1536]{1,0:T(8,128)(2,1)S(1)}, ...), condition=%wide.region_7.8_spmd, body=%wide.region_0.7_spmd.sunk | while | flops 155647696 | bytes 20957296 | solution.py:131
  105.9 5.0 fusion.69
  111.2 13.0 %all_gather.29 = bf16[64,12,128]{2,0,1:T(8,128)(2,1)S(1)} all-gather(bf16[8,12,128]{2,0,1:T(8,128)(2,1)S(1)} %multiply_convert_fusion.4), channel_id=1, replica_groups=mesh['pipe'=4,'seq'=8] {'seq'}, dimensions={0}, use_global_device_ids=true | all-gather | bytes 221184 | tf_op jit(solution)/shard_map/while/body/eval_jaxpr/all_gather | solution.py:94
  127.4 13.0 %all-gather.2 = bf16[64,1,12,128]{3,0,2,1:T(8,128)(2,1)S(1)} all-gather(bf16[8,1,12,128]{3,0,2,1:T(8,128)(2,1)S(1)} %slice.120), channel_id=2, replica_groups=mesh['pipe'=4,'seq'=8] {'seq'}, dimensions={0}, use_global_device_ids=true | all-gather | bytes 221184 | tf_op jit(solution)/shard_map/while/body/eval_jaxpr/all_gather | solution.py:95
  142.0 3.8 select_select_fusion.3
  154.0 5.0 fusion.69
  159.2 13.0 %all_gather.29 = bf16[64,12,128]{2,0,1:T(8,128)(2,1)S(1)} all-gather(bf16[8,12,128]{2,0,1:T(8,128)(2,1)S(1)} %multiply_convert_fusion.4), channel_id=1, replica_groups=mesh['pipe'=4,'seq'=8] {'seq'}, dimensions={0}, use_global_device_ids=true | all-gather | bytes 221184 | tf_op jit(solution)/shard_map/while/body/eval_jaxpr/all_gather | solution.py:94
  175.4 13.0 %all-gather.2 = bf16[64,1,12,128]{3,0,2,1:T(8,128)(2,1)S(1)} all-gather(bf16[8,1,12,128]{3,0,2,1:T(8,128)(2,1)S(1)} %slice.120), channel_id=2, replica_groups=mesh['pipe'=4,'seq'=8] {'seq'}, dimensions={0}, use_global_device_ids=true | all-gather | bytes 221184 | tf_op jit(solution)/shard_map/while/body/eval_jaxpr/all_gather | solution.py:95
  202.0 5.0 fusion.69
  207.3 13.0 %all_gather.29 = bf16[64,12,128]{2,0,1:T(8,128)(2,1)S(1)} all-gather(bf16[8,12,128]{2,0,1:T(8,128)(2,1)S(1)} %multiply_convert_fusion.4), channel_id=1, replica_groups=mesh['pipe'=4,'seq'=8] {'seq'}, dimensions={0}, use_global_device_ids=true | all-gather | bytes 221184 | tf_op jit(solution)/shard_map/while/body/eval_jaxpr/all_gather | solution.py:94
  223.4 13.0 %all-gather.2 = bf16[64,1,12,128]{3,0,2,1:T(8,128)(2,1)S(1)} all-gather(bf16[8,1,12,128]{3,0,2,1:T(8,128)(2,1)S(1)} %slice.120), channel_id=2, replica_groups=mesh['pipe'=4,'seq'=8] {'seq'}, dimensions={0}, use_global_device_ids=true | all-gather | bytes 221184 | tf_op jit(solution)/shard_map/while/body/eval_jaxpr/all_gather | solution.py:95
  250.0 5.0 fusion.69
  255.3 13.0 %all_gather.29 = bf16[64,12,128]{2,0,1:T(8,128)(2,1)S(1)} all-gather(bf16[8,12,128]{2,0,1:T(8,128)(2,1)S(1)} %multiply_convert_fusion.4), channel_id=1, replica_groups=mesh['pipe'=4,'seq'=8] {'seq'}, dimensions={0}, use_global_device_ids=true | all-gather | bytes 221184 | tf_op jit(solution)/shard_map/while/body/eval_jaxpr/all_gather | solution.py:94
  271.4 13.0 %all-gather.2 = bf16[64,1,12,128]{3,0,2,1:T(8,128)(2,1)S(1)} all-gather(bf16[8,1,12,128]{3,0,2,1:T(8,128)(2,1)S(1)} %slice.120), channel_id=2, replica_groups=mesh['pipe'=4,'seq'=8] {'seq'}, dimensions={0}, use_global_device_ids=true | all-gather | bytes 221184 | tf_op jit(solution)/shard_map/while/body/eval_jaxpr/all_gather | solution.py:95
  298.0 5.0 fusion.69
  303.3 13.0 %all_gather.29 = bf16[64,12,128]{2,0,1:T(8,128)(2,1)S(1)} all-gather(bf16[8,12,128]{2,0,1:T(8,128)(2,1)S(1)} %multiply_convert_fusion.4), channel_id=1, replica_groups=mesh['pipe'=4,'seq'=8] {'seq'}, dimensions={0}, use_global_device_ids=true | all-gather | bytes 221184 | tf_op jit(solution)/shard_map/while/body/eval_jaxpr/all_gather | solution.py:94
  319.5 13.0 %all-gather.2 = bf16[64,1,12,128]{3,0,2,1:T(8,128)(2,1)S(1)} all-gather(bf16[8,1,12,128]{3,0,2,1:T(8,128)(2,1)S(1)} %slice.120), channel_id=2, replica_groups=mesh['pipe'=4,'seq'=8] {'seq'}, dimensions={0}, use_global_device_ids=true | all-gather | bytes 221184 | tf_op jit(solution)/shard_map/while/body/eval_jaxpr/all_gather | solution.py:95
  346.1 5.0 fusion.69
  351.3 13.0 %all_gather.29 = bf16[64,12,128]{2,0,1:T(8,128)(2,1)S(1)} all-gather(bf16[8,12,128]{2,0,1:T(8,128)(2,1)S(1)} %multiply_convert_fusion.4), channel_id=1, replica_groups=mesh['pipe'=4,'seq'=8] {'seq'}, dimensions={0}, use_global_device_ids=true | all-gather | bytes 221184 | tf_op jit(solution)/shard_map/while/body/eval_jaxpr/all_gather | solution.py:94
  367.5 13.0 %all-gather.2 = bf16[64,1,12,128]{3,0,2,1:T(8,128)(2,1)S(1)} all-gather(bf16[8,1,12,128]{3,0,2,1:T(8,128)(2,1)S(1)} %slice.120), channel_id=2, replica_groups=mesh['pipe'=4,'seq'=8] {'seq'}, dimensions={0}, use_global_device_ids=true | all-gather | bytes 221184 | tf_op jit(solution)/shard_map/while/body/eval_jaxpr/all_gather | solution.py:95
  394.1 5.0 fusion.69
  399.4 13.0 %all_gather.29 = bf16[64,12,128]{2,0,1:T(8,128)(2,1)S(1)} all-gather(bf16[8,12,128]{2,0,1:T(8,128)(2,1)S(1)} %multiply_convert_fusion.4), channel_id=1, replica_groups=mesh['pipe'=4,'seq'=8] {'seq'}, dimensions={0}, use_global_device_ids=true | all-gather | bytes 221184 | tf_op jit(solution)/shard_map/while/body/eval_jaxpr/all_gather | solution.py:94
  415.5 13.0 %all-gather.2 = bf16[64,1,12,128]{3,0,2,1:T(8,128)(2,1)S(1)} all-gather(bf16[8,1,12,128]{3,0,2,1:T(8,128)(2,1)S(1)} %slice.120), channel_id=2, replica_groups=mesh['pipe'=4,'seq'=8] {'seq'}, dimensions={0}, use_global_device_ids=true | all-gather | bytes 221184 | tf_op jit(solution)/shard_map/while/body/eval_jaxpr/all_gather | solution.py:95
  442.1 5.0 fusion.69
  447.4 13.0 %all_gather.29 = bf16[64,12,128]{2,0,1:T(8,128)(2,1)S(1)} all-gather(bf16[8,12,128]{2,0,1:T(8,128)(2,1)S(1)} %multiply_convert_fusion.4), channel_id=1, replica_groups=mesh['pipe'=4,'seq'=8] {'seq'}, dimensions={0}, use_global_device_ids=true | all-gather | bytes 221184 | tf_op jit(solution)/shard_map/while/body/eval_jaxpr/all_gather | solution.py:94
  463.6 13.0 %all-gather.2 = bf16[64,1,12,128]{3,0,2,1:T(8,128)(2,1)S(1)} all-gather(bf16[8,1,12,128]{3,0,2,1:T(8,128)(2,1)S(1)} %slice.120), channel_id=2, replica_groups=mesh['pipe'=4,'seq'=8] {'seq'}, dimensions={0}, use_global_device_ids=true | all-gather | bytes 221184 | tf_op jit(solution)/shard_map/while/body/eval_jaxpr/all_gather | solution.py:95
  490.2 5.0 fusion.69
  495.4 13.0 %all_gather.29 = bf16[64,12,128]{2,0,1:T(8,128)(2,1)S(1)} all-gather(bf16[8,12,128]{2,0,1:T(8,128)(2,1)S(1)} %multiply_convert_fusion.4), channel_id=1, replica_groups=mesh['pipe'=4,'seq'=8] {'seq'}, dimensions={0}, use_global_device_ids=true | all-gather | bytes 221184 | tf_op jit(solution)/shard_map/while/body/eval_jaxpr/all_gather | solution.py:94
  511.6 13.0 %all-gather.2 = bf16[64,1,12,128]{3,0,2,1:T(8,128)(2,1)S(1)} all-gather(bf16[8,1,12,128]{3,0,2,1:T(8,128)(2,1)S(1)} %slice.120), channel_id=2, replica_groups=mesh['pipe'=4,'seq'=8] {'seq'}, dimensions={0}, use_global_device_ids=true | all-gather | bytes 221184 | tf_op jit(solution)/shard_map/while/body/eval_jaxpr/all_gather | solution.py:95
  534.7 14.7 %psum.7 = bf16[2,8,1536]{2,1,0:T(8,128)(2,1)S(1)} all-reduce(bf16[2,8,1536]{2,1,0:T(8,128)(2,1)S(1)} %broadcast_select_fusion), channel_id=1, replica_groups=mesh['pipe'=4,'seq'=8] {'pipe'}, use_global_device_ids=true, to_apply=%region_8.9 | all-reduce | flops 24576 | bytes 98304 | tf_op jit(solution)/shard_map/psum | solution.py:19
  (231 shorter events, 151.0 us)
Async XLA Ops:
  6.5 95.9 %all-gather.5.cloned.1.call-start = ((), (), s32[]{:S(2)}) async-start(), calls=%async_computation | async-start | bytes 10616832 | tf_op jit(solution)/shard_map/all_gather | solution.py:66
  111.0 29.3 %copy-start.1 = (f32[16]{0:T(128)S(1)}, f32[16]{0:T(128)}, u32[]{:S(2)}) copy-start(f32[16]{0:T(128)} %get-tuple-element.560) | copy-start | bytes 196 | tf_op jit(solution)/shard_map/while
  124.2 23.1 %copy-start = (s32[3]{0:T(128)S(1)}, s32[3]{0:T(128)}, u32[]{:S(2)}) copy-start(s32[3]{0:T(128)} %get-tuple-element.575) | copy-start | bytes 40 | tf_op jit(solution)/shard_map/while
  145.7 4.8 collective-permute-start
  159.0 29.3 %copy-start.1 = (f32[16]{0:T(128)S(1)}, f32[16]{0:T(128)}, u32[]{:S(2)}) copy-start(f32[16]{0:T(128)} %get-tuple-element.560) | copy-start | bytes 196 | tf_op jit(solution)/shard_map/while
  172.2 22.2 %copy-start = (s32[3]{0:T(128)S(1)}, s32[3]{0:T(128)}, u32[]{:S(2)}) copy-start(s32[3]{0:T(128)} %get-tuple-element.575) | copy-start | bytes 40 | tf_op jit(solution)/shard_map/while
  193.8 4.8 collective-permute-start
  207.0 29.3 %copy-start.1 = (f32[16]{0:T(128)S(1)}, f32[16]{0:T(128)}, u32[]{:S(2)}) copy-start(f32[16]{0:T(128)} %get-tuple-element.560) | copy-start | bytes 196 | tf_op jit(solution)/shard_map/while
  220.2 21.9 %copy-start = (s32[3]{0:T(128)S(1)}, s32[3]{0:T(128)}, u32[]{:S(2)}) copy-start(s32[3]{0:T(128)} %get-tuple-element.575) | copy-start | bytes 40 | tf_op jit(solution)/shard_map/while
  241.8 4.8 collective-permute-start
  255.1 29.3 %copy-start.1 = (f32[16]{0:T(128)S(1)}, f32[16]{0:T(128)}, u32[]{:S(2)}) copy-start(f32[16]{0:T(128)} %get-tuple-element.560) | copy-start | bytes 196 | tf_op jit(solution)/shard_map/while
  268.2 21.9 %copy-start = (s32[3]{0:T(128)S(1)}, s32[3]{0:T(128)}, u32[]{:S(2)}) copy-start(s32[3]{0:T(128)} %get-tuple-element.575) | copy-start | bytes 40 | tf_op jit(solution)/shard_map/while
  289.8 4.8 collective-permute-start
  303.1 29.3 %copy-start.1 = (f32[16]{0:T(128)S(1)}, f32[16]{0:T(128)}, u32[]{:S(2)}) copy-start(f32[16]{0:T(128)} %get-tuple-element.560) | copy-start | bytes 196 | tf_op jit(solution)/shard_map/while
  316.3 21.9 %copy-start = (s32[3]{0:T(128)S(1)}, s32[3]{0:T(128)}, u32[]{:S(2)}) copy-start(s32[3]{0:T(128)} %get-tuple-element.575) | copy-start | bytes 40 | tf_op jit(solution)/shard_map/while
  337.8 4.8 collective-permute-start
  351.1 29.3 %copy-start.1 = (f32[16]{0:T(128)S(1)}, f32[16]{0:T(128)}, u32[]{:S(2)}) copy-start(f32[16]{0:T(128)} %get-tuple-element.560) | copy-start | bytes 196 | tf_op jit(solution)/shard_map/while
  364.3 21.9 %copy-start = (s32[3]{0:T(128)S(1)}, s32[3]{0:T(128)}, u32[]{:S(2)}) copy-start(s32[3]{0:T(128)} %get-tuple-element.575) | copy-start | bytes 40 | tf_op jit(solution)/shard_map/while
  385.9 4.8 collective-permute-start
  399.2 29.3 %copy-start.1 = (f32[16]{0:T(128)S(1)}, f32[16]{0:T(128)}, u32[]{:S(2)}) copy-start(f32[16]{0:T(128)} %get-tuple-element.560) | copy-start | bytes 196 | tf_op jit(solution)/shard_map/while
  412.3 21.9 %copy-start = (s32[3]{0:T(128)S(1)}, s32[3]{0:T(128)}, u32[]{:S(2)}) copy-start(s32[3]{0:T(128)} %get-tuple-element.575) | copy-start | bytes 40 | tf_op jit(solution)/shard_map/while
  433.9 4.8 collective-permute-start
  447.2 29.3 %copy-start.1 = (f32[16]{0:T(128)S(1)}, f32[16]{0:T(128)}, u32[]{:S(2)}) copy-start(f32[16]{0:T(128)} %get-tuple-element.560) | copy-start | bytes 196 | tf_op jit(solution)/shard_map/while
  460.4 21.9 %copy-start = (s32[3]{0:T(128)S(1)}, s32[3]{0:T(128)}, u32[]{:S(2)}) copy-start(s32[3]{0:T(128)} %get-tuple-element.575) | copy-start | bytes 40 | tf_op jit(solution)/shard_map/while
  481.9 4.8 collective-permute-start
  495.2 29.3 %copy-start.1 = (f32[16]{0:T(128)S(1)}, f32[16]{0:T(128)}, u32[]{:S(2)}) copy-start(f32[16]{0:T(128)} %get-tuple-element.560) | copy-start | bytes 196 | tf_op jit(solution)/shard_map/while
  508.4 21.9 %copy-start = (s32[3]{0:T(128)S(1)}, s32[3]{0:T(128)}, u32[]{:S(2)}) copy-start(s32[3]{0:T(128)} %get-tuple-element.575) | copy-start | bytes 40 | tf_op jit(solution)/shard_map/while
  530.0 4.8 collective-permute-start
Sparse Core Ops, SparseCore 0:
  9.0 93.4 all-gather.4
where the time goes:
time: 559 us; the launch traced here: 557 us
  blocking collectives  258 us (46%)
  matrix products  128 us (23%)
  waiting for transfers between devices  106 us (19%)
  other arithmetic  34 us (6%)
  between operations  13.4 us (2%)
  local copies, waits for them, and re-layouts  13 us (2%)
    all_gather x9, blocking collectives, apply_layer(): lax.all_gather(value_rows, 'seq', axis=0, tiled=True)  117 us
    all_gather x9, blocking collectives, apply_layer(): lax.all_gather(key_rows, 'seq', axis=0, tiled=True)  117 us
    all_gather x1, waiting for transfers between devices, shards(): kv_weight = lax.all_gather(w_kv, 'seq', axis=1, tiled=True)[0]  84.6 us
    dot_general x9, matrix products, key_value(): projected = jnp.dot(modded, kv_weight, preferred_element_type=jnp.float32)  45.4 us
    dot_general x9, matrix products, apply_layer(): jnp.dot(attended, out_weight, preferred_element_type=jnp.float32)  34 us
    dot_general x9, matrix products, apply_layer(): queries = jnp.dot(modded, query_weight, preferred_element_type=jnp.float32)  28.6 us
    ppermute x9, waiting for transfers between devices, passed_along(): return lax.ppermute(value, axis, pairs)  20.2 us
    dot_general x9, matrix products, apply_layer(): modulation = jnp.dot(one_hot, mod_rows, precision=lax.Precision.HIGHEST)  16.5 us
  transfers between devices with their start and end apart: 10, of which 10 were waited for; matrix products, arithmetic and copies ran while one was open for 3% of the time, Pallas kernels for 0%

commit v1 on v0

v1 whole, which is shorter than its diff:
```python
import functools
import math

import jax
import jax.numpy as jnp
from jax import lax
from jax.experimental import pallas as pl
from jax.experimental.pallas import tpu as pltpu
from jax.sharding import PartitionSpec as P

norm_eps = 1e-06
MESH = pl.DeviceIdType.MESH


def rms_rows(values, gain_row):
    mean_square = jnp.mean(values * values, axis=-1, keepdims=True)
    return (values * lax.rsqrt(mean_square + norm_eps) * gain_row).astype(jnp.bfloat16)


def kernel(
    n_pipe, n_seq, groups, micro, steps, head_dim,
    lat_ref, ts_ref, ss_ref, mod_ref, gain_ref, wq_hbm, wkv_hbm, wo_hbm,
    out_ref,
    wq, wk, wv, wo, latbuf, hid, att, outb, prev, modded, fin_src, fin,
    local_sem, kv_recv, kv_send, kv_fwd, lat_send, lat_recv,
    hid_recv, hid_send, hid_fwd, att_recv, att_send, fin_send, fin_recv,
):
    sharers = n_seq // groups
    rows, share = lat_ref.shape[1], lat_ref.shape[2]
    tokens = rows * n_seq
    width = share * n_pipe
    block = wq.shape[1]
    inner = block * groups
    depth = wkv_hbm.shape[1]
    part = tokens // sharers
    per_block = n_pipe // groups
    per_part = n_seq // sharers
    heads = block // head_dim
    score_scale = 1.0 / math.sqrt(head_dim)
    last = n_pipe - 1

    pipe, seq = lax.axis_index("pipe"), lax.axis_index("seq")
    mine, sharer = seq // sharers, seq % sharers

    def remote(src, dst, send, recv, to_pipe, to_seq):
        return pltpu.make_async_remote_copy(
            src_ref=src, dst_ref=dst, send_sem=send, recv_sem=recv,
            device_id=(to_pipe, to_seq), device_id_type=MESH,
        )

    def lat_copy(to_pipe, to_seq, index):
        return remote(lat_ref, latbuf.at[pipe, seq], lat_send.at[index],
                      lat_recv.at[pipe, seq], to_pipe, to_seq)

    def lat_local():
        return pltpu.make_async_copy(lat_ref, latbuf.at[pipe, seq], lat_recv.at[pipe, seq])

    def lat_arrived(from_pipe, from_seq):
        pltpu.make_async_copy(lat_ref, latbuf.at[from_pipe, from_seq],
                              lat_recv.at[from_pipe, from_seq]).wait()

    keeper = (pipe // per_block) * sharers + seq // per_part
    for ahead in range(n_seq):
        target = lax.rem(seq + ahead, n_seq)
        if ahead == 0:
            @pl.when(pipe == 0)
            def _():
                lat_local().start()

            @pl.when(pipe != 0)
            def _():
                lat_copy(0, target, ahead).start()
        else:
            lat_copy(0, target, ahead).start()
    keeps_own = (pipe == last) & (keeper == seq)

    @pl.when(keeps_own)
    def _():
        lat_local().start()

    @pl.when(jnp.logical_not(keeps_own))
    def _():
        lat_copy(last, keeper, n_seq).start()

    wkv = (wk, wv)

    def columns(kv, group):
        start = pl.multiple_of(kv * inner + group * block, 128)
        return wkv_hbm.at[0, :, pl.ds(start, block)]

    def slab(kv, owner):
        return wkv[kv].at[pl.ds(pl.multiple_of(owner * depth, 16), depth), :]

    def kv_copy(kv, ahead):
        group = lax.rem(mine + ahead, groups)
        return remote(columns(kv, group), slab(kv, seq), kv_send.at[kv, ahead],
                      kv_recv.at[kv, seq], pipe, group * sharers + sharer)

    def kv_pass(kv, ahead, step):
        group = lax.rem(mine + ahead, groups)
        owner = group * sharers + sharer
        source = columns(kv, mine) if ahead == 0 else slab(kv, owner)
        return remote(source, slab(kv, owner), kv_fwd.at[kv, ahead, step],
                      kv_recv.at[kv, owner], pipe, mine * sharers + lax.rem(sharer + step, sharers))

    def kv_arrived(kv, owner):
        pltpu.make_async_copy(columns(kv, mine), slab(kv, owner), kv_recv.at[kv, owner]).wait()

    own_columns = pl.ds(pl.multiple_of(mine * block, 128), block)
    copy_q = pltpu.make_async_copy(wq_hbm.at[0, :, own_columns], wq, local_sem.at[0])
    copy_o = pltpu.make_async_copy(wo_hbm.at[0, :, own_columns], wo, local_sem.at[1])
    for kv in range(2):
        for ahead in range(groups - 1, 0, -1):
            kv_copy(kv, ahead).start()
    for kv in range(2):
        pltpu.make_async_copy(columns(kv, mine), slab(kv, seq), kv_recv.at[kv, seq]).start()
        for step in range(1, sharers):
            kv_pass(kv, 0, step).start()
    copy_q.start()
    copy_o.start()
    for kv in range(2):
        for ahead in range(1, groups):
            kv_arrived(kv, lax.rem(mine + ahead, groups) * sharers + sharer)
            for step in range(1, sharers):
                kv_pass(kv, ahead, step).start()
    for kv in range(2):
        kv_arrived(kv, seq)
        for step in range(1, sharers):
            for group in range(groups):
                kv_arrived(kv, group * sharers + lax.rem(sharer + step, sharers))
    copy_q.wait()
    copy_o.wait()

    @pl.when(pipe == 0)
    def _():
        for from_pipe in range(n_pipe):
            for from_seq in range(n_seq):
                lat_arrived(from_pipe, from_seq)

    @pl.when(pipe == last)
    def _():
        for slot in range(micro):
            pieces = []
            for wide in range(per_block):
                pieces.append(jnp.concatenate([
                    latbuf_wait_load(latbuf, lat_arrived, slot == 0, mine * per_block + wide,
                                     sharer * per_part + index, slot)
                    for index in range(per_part)
                ], axis=0))
            prev[slot] = jnp.concatenate(pieces, axis=1) if per_block > 1 else pieces[0]

    def hid_send_copy(step, slot, group):
        at_last = pipe == last
        to_step = step + jnp.where(at_last, 1, 0)
        return remote(outb.at[step, slot], hid.at[to_step, slot, mine, sharer],
                      hid_send.at[step, slot, group], hid_recv.at[to_step, slot, mine, sharer],
                      lax.rem(pipe + 1, n_pipe), group * sharers + sharer)

    def hid_pass(step, slot, group, ahead):
        return remote(hid.at[step, slot, group, sharer], hid.at[step, slot, group, sharer],
                      hid_fwd.at[step, slot, group, ahead], hid_recv.at[step, slot, group, sharer],
                      pipe, mine * sharers + lax.rem(sharer + ahead, sharers))

    def hid_arrived(step, slot, group, from_sharer):
        pltpu.make_async_copy(outb.at[step, slot], hid.at[step, slot, group, from_sharer],
                              hid_recv.at[step, slot, group, from_sharer]).wait()

    def att_copy(step, slot, ahead):
        group = lax.rem(mine + ahead, groups)
        return remote(att.at[step, slot, mine], att.at[step, slot, mine],
                      att_send.at[step, slot, ahead], att_recv.at[step, slot, mine],
                      pipe, group * sharers + sharer)

    def att_arrived(step, slot, ahead):
        group = lax.rem(mine + ahead, groups)
        pltpu.make_async_copy(att.at[step, slot, mine], att.at[step, slot, group],
                              att_recv.at[step, slot, group]).wait()

    def fin_targets(slot):
        for wide in range(per_block):
            for index in range(per_part):
                to_pipe, to_seq = mine * per_block + wide, sharer * per_part + index
                source = fin_src.at[slot, wide, pl.ds(index * rows, rows), :]
                yield to_pipe, to_seq, source, fin_send.at[slot, wide, index]

    def visit(item, carry):
        step, slot = item // micro, item % micro
        tau = ts_ref[step, slot]
        from_latents = (pipe == 0) & (step == 0)

        @pl.when(from_latents)
        def _():
            for group in range(groups):
                pieces = []
                for wide in range(per_block):
                    pieces.append(jnp.concatenate([
                        latbuf[group * per_block + wide, index, slot].astype(jnp.float32)
                        for index in range(n_seq)
                    ], axis=0))
                whole = jnp.concatenate(pieces, axis=1) if per_block > 1 else pieces[0]
                for at in range(sharers):
                    hid[0, slot, group, at] = whole[at * part:(at + 1) * part].astype(jnp.bfloat16)

        @pl.when(jnp.logical_not(from_latents))
        def _():
            for group in range(groups):
                hid_arrived(step, slot, group, sharer)
                for ahead in range(1, sharers):
                    hid_pass(step, slot, group, ahead).start()
            for group in range(groups):
                for ahead in range(1, sharers):
                    hid_arrived(step, slot, group, lax.rem(sharer + ahead, sharers))

        as_float = jnp.concatenate([
            jnp.concatenate([hid[step, slot, group, at].astype(jnp.float32) for at in range(sharers)], axis=0)
            for group in range(groups)
        ], axis=1)
        center = jnp.mean(as_float, axis=-1, keepdims=True)
        away = as_float - center
        spread = jnp.mean(away * away, axis=-1, keepdims=True)
        shift_row = mod_ref[0, pl.ds(tau, 1), 0:width]
        scale_row = mod_ref[0, pl.ds(tau, 1), width:2 * width]
        modded[...] = (
            away * lax.rsqrt(spread + norm_eps) * (1.0 + scale_row) + shift_row
        ).astype(jnp.bfloat16)
        queries = jnp.dot(modded[pl.ds(pl.multiple_of(sharer * part, 16), part), :], wq[...],
                          preferred_element_type=jnp.float32)
        keys = jnp.dot(modded[...], wk[...], preferred_element_type=jnp.float32)
        values = jnp.dot(modded[...], wv[...], preferred_element_type=jnp.float32).astype(jnp.bfloat16)
        gain_query, gain_key = gain_ref[0, 0:1, :], gain_ref[0, 1:2, :]
        for head in range(heads):
            here = slice(head * head_dim, (head + 1) * head_dim)
            logits = lax.dot_general(
                rms_rows(queries[:, here], gain_query), rms_rows(keys[:, here], gain_key),
                (((1,), (1,)), ((), ())), preferred_element_type=jnp.float32,
            ) * score_scale
            weights = jnp.exp(logits)
            total = jnp.sum(weights, axis=-1, keepdims=True)
            weighted = jnp.dot(weights.astype(jnp.bfloat16), values[:, here],
                               preferred_element_type=jnp.float32)
            att[step, slot, mine, :, here] = (weighted / total).astype(jnp.bfloat16)
        for ahead in range(1, groups):
            att_copy(step, slot, ahead).start()
        gate_row = mod_ref[0, pl.ds(tau, 1), pl.ds(pl.multiple_of(2 * width + mine * block, 128), block)]
        residual = hid[step, slot, mine, sharer].astype(jnp.float32)
        for ahead in range(1, groups):
            att_arrived(step, slot, ahead)
        attended = jnp.concatenate([att[step, slot, group] for group in range(groups)], axis=1)
        projected = jnp.dot(attended, wo[...], preferred_element_type=jnp.float32)
        layer_out = (residual + gate_row * projected).astype(jnp.bfloat16)
        ends = (pipe == last) & (step == steps - 1)

        @pl.when(pipe != last)
        def _():
            outb[step, slot] = layer_out

        @pl.when(pipe == last)
        def _():
            update = (prev[slot] - ss_ref[tau] * layer_out.astype(jnp.float32)).astype(jnp.bfloat16)
            outb[step, slot] = update
            prev[slot] = update.astype(jnp.float32)

        @pl.when(jnp.logical_not(ends))
        def _():
            for ahead in range(groups):
                hid_send_copy(step, slot, lax.rem(mine + ahead, groups)).start()

        @pl.when(ends)
        def _():
            update = prev[slot]
            for wide in range(per_block):
                fin_src[slot, wide] = update[:, wide * share:(wide + 1) * share]
            for to_pipe, to_seq, source, send in fin_targets(slot):
                own = (to_pipe == pipe) & (to_seq == seq)

                @pl.when(own)
                def _():
                    pltpu.make_async_copy(source, fin.at[slot], fin_recv.at[slot]).start()

                @pl.when(jnp.logical_not(own))
                def _():
                    remote(source, fin.at[slot], send, fin_recv.at[slot], to_pipe, to_seq).start()
        return carry

    lax.fori_loop(0, micro * steps, visit, 0)

    for slot in range(micro):
        pltpu.make_async_copy(fin_src.at[slot, 0, pl.ds(0, rows), :], fin.at[slot],
                              fin_recv.at[slot]).wait()
        out_ref[slot] = fin[slot].astype(jnp.bfloat16)

    for ahead in range(n_seq):
        target = lax.rem(seq + ahead, n_seq)
        if ahead == 0:
            @pl.when(pipe != 0)
            def _():
                lat_copy(0, target, ahead).wait_send()
        else:
            lat_copy(0, target, ahead).wait_send()

    @pl.when(jnp.logical_not(keeps_own))
    def _():
        lat_copy(last, keeper, n_seq).wait_send()

    for kv in range(2):
        for ahead in range(1, groups):
            kv_copy(kv, ahead).wait_send()
        for ahead in range(groups):
            for step in range(1, sharers):
                kv_pass(kv, ahead, step).wait_send()

    def drain(item, carry):
        step, slot = item // micro, item % micro
        ends = (pipe == last) & (step == steps - 1)
        for ahead in range(1, groups):
            att_copy(step, slot, ahead).wait_send()

        @pl.when(jnp.logical_not((pipe == 0) & (step == 0)))
        def _():
            for group in range(groups):
                for ahead in range(1, sharers):
                    hid_pass(step, slot, group, ahead).wait_send()

        @pl.when(jnp.logical_not(ends))
        def _():
            for group in range(groups):
                hid_send_copy(step, slot, group).wait_send()

        @pl.when(ends)
        def _():
            for to_pipe, to_seq, source, send in fin_targets(slot):
                @pl.when(jnp.logical_not((to_pipe == pipe) & (to_seq == seq)))
                def _():
                    remote(source, fin.at[slot], send, fin_recv.at[slot], to_pipe, to_seq).wait_send()
        return carry

    lax.fori_loop(0, micro * steps, drain, 0)


def latbuf_wait_load(latbuf, lat_arrived, first, from_pipe, from_seq, slot):
    if first:
        lat_arrived(from_pipe, from_seq)
    return latbuf[from_pipe, from_seq, slot].astype(jnp.float32)


def shards(latents, timesteps, step_sizes, mod_table, qk_gain, w_query, w_kv, w_out):
    n_pipe, n_seq = lax.axis_size("pipe"), lax.axis_size("seq")
    micro, rows, share = latents.shape
    steps = timesteps.shape[0]
    head_dim = qk_gain.shape[2]
    width, inner = w_query.shape[1], w_query.shape[2]
    heads = inner // head_dim
    groups = math.gcd(math.gcd(heads, n_seq), n_pipe)
    while n_seq // groups < 2:
        groups //= 2
    sharers = n_seq // groups
    block = inner // groups
    part = rows * n_seq // sharers
    per_block, per_part = n_pipe // groups, n_seq // sharers
    bf16, f32 = jnp.bfloat16, jnp.float32
    vmem = pl.BlockSpec(memory_space=pltpu.VMEM)
    smem = pl.BlockSpec(memory_space=pltpu.SMEM)
    hbm = pl.BlockSpec(memory_space=pl.ANY)
    dma = pltpu.SemaphoreType.DMA
    return pl.pallas_call(
        functools.partial(kernel, n_pipe, n_seq, groups, micro, steps, head_dim),
        out_shape=jax.ShapeDtypeStruct(latents.shape, bf16),
        in_specs=[vmem, smem, smem, vmem, vmem, hbm, hbm, hbm],
        out_specs=vmem,
        scratch_shapes=[
            pltpu.VMEM((width, block), bf16),
            pltpu.VMEM((width, block), bf16),
            pltpu.VMEM((width, block), bf16),
            pltpu.VMEM((inner, block), bf16),
            pltpu.VMEM((n_pipe, n_seq, micro, rows, share), bf16),
            pltpu.VMEM((steps, micro, groups, sharers, part, block), bf16),
            pltpu.VMEM((steps, micro, groups, part, block), bf16),
            pltpu.VMEM((steps, micro, part, block), bf16),
            pltpu.VMEM((micro, part, block), f32),
            pltpu.VMEM((rows * n_seq, width), bf16),
            pltpu.VMEM((micro, per_block, part, share), f32),
            pltpu.VMEM((micro, rows, share), f32),
            dma((2,)),
            dma((2, n_seq)),
            dma((2, groups)),
            dma((2, groups, sharers)),
            dma((n_seq + 1,)),
            dma((n_pipe, n_seq)),
            dma((steps, micro, groups, sharers)),
            dma((steps, micro, groups)),
            dma((steps, micro, groups, sharers)),
            dma((steps, micro, groups)),
            dma((steps, micro, groups)),
            dma((micro, per_block, per_part)),
            dma((micro,)),
        ],
        compiler_params=pltpu.CompilerParams(
            has_side_effects=True, vmem_limit_bytes=48 * 1024 * 1024
        ),
        cost_estimate=pl.CostEstimate(
            flops=2 * 4 * rows * n_seq * width * block * micro * steps,
            bytes_accessed=2 * 4 * width * block, transcendentals=0,
        ),
        name="denoise",
    )(latents, timesteps, step_sizes, mod_table, qk_gain, w_query, w_kv, w_out)


def solution(mesh):
    in_specs = (
        P(None, "seq", "pipe"),
        P(),
        P(),
        P("pipe", None, None),
        P("pipe", None, None),
        P("pipe", None, None),
        P("pipe", "seq", None),
        P("pipe", None, None),
    )
    out_specs = P(None, "seq", "pipe")
    return jax.shard_map(shards, mesh=mesh, in_specs=in_specs, out_specs=out_specs, check_vma=False)
```

time: 559 us -> 143 us (0.26)
  blocking collectives: 258 us -> 0 us
  Pallas kernels: 0 us -> 137 us
  matrix products: 128 us -> 0 us
  waiting for transfers between devices: 106 us -> 0 us
  other arithmetic: 34 us -> 0 us
  between operations: 13.4 us -> 0.02 us
  local copies, waits for them, and re-layouts: 13 us -> 5.55 us
    all_gather x19 -> x0, blocking collectives: 243 us -> none  [the longest x9 117 us: apply_layer(): lax.all_gather(value_rows, 'seq', axis=0, tiled=True)]
    pallas_call x0 -> x1, Pallas kernels: none -> 137 us  [shards(): pl.pallas_call(functools.partial(kernel, n_pipe, n_seq, groups, micro, st...]
    dot_general x45 -> x0, matrix products: 128 us -> none  [the longest x9 45.4 us: key_value(): projected = jnp.dot(modded, kv_weight, preferred_element_type=jnp.float32)]
    all_gather x1 -> x0, waiting for transfers between devices: 84.6 us -> none  [shards(): kv_weight = lax.all_gather(w_kv, 'seq', axis=1, tiled=True)[0]]
    ppermute x9 -> x0, waiting for transfers between devices: 20.2 us -> none  [passed_along(): return lax.ppermute(value, axis, pairs)]
    psum x1 -> x0, blocking collectives: 14.7 us -> none  [from_root(): return lax.psum(kept, axis)]
    dynamic_slice x19 -> x0, local copies, waits for them, and re-layouts: 12.2 us -> none  [the longest x9 11.5 us: advance(): time_index = timesteps[step_safe, slot_safe]]
    dot_general x9 -> x0, other arithmetic: 11.5 us -> none  [advance(): step_size = jnp.dot(one_hot, step_sizes, precision=lax.Precision.HIGHEST)]
  transfers between devices with their start and end apart: 10 -> 0, of which waited for: 10 -> 0; matrix products, arithmetic and copies ran while one was open for 3% -> 0% of each run, Pallas kernels for 0% -> 0%
where the time goes in v1:
time: 143 us
  Pallas kernels  137 us (96%)
  local copies, waits for them, and re-layouts  5.55 us (4%)
    pallas_call x1, Pallas kernels, shards(): pl.pallas_call(functools.partial(kernel, n_pipe, n_seq, groups, micro, st...  137 us
    unnamed x13, local copies, waits for them, and re-layouts  5.55 us

profile of v1, /device:TPU:0, one launch (start us, length us, event | category | flops | bytes accessed | tf_op | source)
XLA Modules:
  0.0 143.0 jit_solution(7532816622663902390)
XLA Ops:
  0.0 0.0 copy-start
  0.0 1.3 copy-done
  1.3 0.0 copy-start.1
  1.3 1.0 copy-done.1
  2.2 0.0 copy-start.2
  2.2 0.7 copy-done.2
  2.9 0.0 copy-start.3
  2.9 0.7 copy-done.3
  3.6 0.0 copy-start.4
  3.6 0.7 copy-done.4
  4.3 0.0 copy-start.5
  4.3 0.7 copy-done.5
  5.0 137.5 %denoise.1 = bf16[2,8,384]{2,1,0:T(8,128)(2,1)S(1)} custom-call(bf16[2,8,384]{2,1,0:T(8,128)(2,1)S(1)} %copy-done.2, s32[2,2]{1,0:T(2,128)S(1)} %copy-done.3, f32[16]{0:T(128)S(1)} %copy-done.5, f32[1,16,4608]{2,1,0:T(8,128)S(1)} %copy-done.1, f32[1,2,128]{2,1,0:T(2,128)S(1)} %copy-done.4, bf16[1,1536,1536]{2,1,0:T(8,128)(2,1)} %wq_hbm.1, ...), custom_call_target="tpu_custom_call" | custom-call | flops 1207959552 | bytes 4718592 | tf_op jit(solution)/shard_map/denoise/pallas_call | solution.py:365
  142.4 0.6 copy.10
Async XLA Ops:
  0.0 1.3 copy-start
  1.3 1.0 copy-start.1
  2.2 0.7 copy-start.2
  2.9 0.7 copy-start.3
  3.6 0.7 copy-start.4
  4.3 0.7 copy-start.5

commit v2 on v1

--- a/solution.py
+++ b/solution.py
@@ -19,9 +19,9 @@
 
 def kernel(
     n_pipe, n_seq, groups, micro, steps, head_dim,
-    lat_ref, ts_ref, ss_ref, mod_ref, gain_ref, wq_hbm, wkv_hbm, wo_hbm,
+    lat_ref, ts_hbm, ss_hbm, mod_hbm, gain_hbm, wq_hbm, wkv_hbm, wo_hbm,
     out_ref,
-    wq, wk, wv, wo, latbuf, hid, att, outb, prev, modded, fin_src, fin,
+    ts_ref, ss_ref, mod_ref, gain_ref, wq, wk, wv, wo, latbuf, hid, att, outb, prev, modded, fin_src, fin,
     local_sem, kv_recv, kv_send, kv_fwd, lat_send, lat_recv,
     hid_recv, hid_send, hid_fwd, att_recv, att_send, fin_send, fin_recv,
 ):
@@ -116,8 +116,15 @@
         pltpu.make_async_copy(columns(kv, mine), slab(kv, seq), kv_recv.at[kv, seq]).start()
         for step in range(1, sharers):
             kv_pass(kv, 0, step).start()
-    copy_q.start()
-    copy_o.start()
+    locals_in = [
+        copy_q, copy_o,
+        pltpu.make_async_copy(ts_hbm, ts_ref, local_sem.at[2]),
+        pltpu.make_async_copy(ss_hbm, ss_ref, local_sem.at[3]),
+        pltpu.make_async_copy(mod_hbm, mod_ref, local_sem.at[4]),
+        pltpu.make_async_copy(gain_hbm, gain_ref, local_sem.at[5]),
+    ]
+    for copy in locals_in:
+        copy.start()
     for kv in range(2):
         for ahead in range(1, groups):
             kv_arrived(kv, lax.rem(mine + ahead, groups) * sharers + sharer)
@@ -128,8 +135,8 @@
         for step in range(1, sharers):
             for group in range(groups):
                 kv_arrived(kv, group * sharers + lax.rem(sharer + step, sharers))
-    copy_q.wait()
-    copy_o.wait()
+    for copy in locals_in:
+        copy.wait()
 
     @pl.when(pipe == 0)
     def _():
@@ -165,16 +172,16 @@
         pltpu.make_async_copy(outb.at[step, slot], hid.at[step, slot, group, from_sharer],
                               hid_recv.at[step, slot, group, from_sharer]).wait()
 
-    def att_copy(step, slot, ahead):
+    def att_copy(step, slot, head, ahead):
         group = lax.rem(mine + ahead, groups)
-        return remote(att.at[step, slot, mine], att.at[step, slot, mine],
-                      att_send.at[step, slot, ahead], att_recv.at[step, slot, mine],
+        return remote(att.at[step, slot, mine, head], att.at[step, slot, mine, head],
+                      att_send.at[step, slot, head, ahead], att_recv.at[step, slot, mine, head],
                       pipe, group * sharers + sharer)
 
-    def att_arrived(step, slot, ahead):
+    def att_arrived(step, slot, head, ahead):
         group = lax.rem(mine + ahead, groups)
-        pltpu.make_async_copy(att.at[step, slot, mine], att.at[step, slot, group],
-                              att_recv.at[step, slot, group]).wait()
+        pltpu.make_async_copy(att.at[step, slot, mine, head], att.at[step, slot, group, head],
+                              att_recv.at[step, slot, group, head]).wait()
 
     def fin_targets(slot):
         for wide in range(per_block):
@@ -183,8 +190,7 @@
                 source = fin_src.at[slot, wide, pl.ds(index * rows, rows), :]
                 yield to_pipe, to_seq, source, fin_send.at[slot, wide, index]
 
-    def visit(item, carry):
-        step, slot = item // micro, item % micro
+    def first_half(step, slot):
         tau = ts_ref[step, slot]
         from_latents = (pipe == 0) & (step == 0)
 
@@ -238,15 +244,23 @@
             total = jnp.sum(weights, axis=-1, keepdims=True)
             weighted = jnp.dot(weights.astype(jnp.bfloat16), values[:, here],
                                preferred_element_type=jnp.float32)
-            att[step, slot, mine, :, here] = (weighted / total).astype(jnp.bfloat16)
-        for ahead in range(1, groups):
-            att_copy(step, slot, ahead).start()
+            att[step, slot, mine, head] = (weighted / total).astype(jnp.bfloat16)
+            for ahead in range(1, groups):
+                att_copy(step, slot, head, ahead).start()
+
+    def second_half(step, slot):
+        tau = ts_ref[step, slot]
         gate_row = mod_ref[0, pl.ds(tau, 1), pl.ds(pl.multiple_of(2 * width + mine * block, 128), block)]
         residual = hid[step, slot, mine, sharer].astype(jnp.float32)
-        for ahead in range(1, groups):
-            att_arrived(step, slot, ahead)
-        attended = jnp.concatenate([att[step, slot, group] for group in range(groups)], axis=1)
-        projected = jnp.dot(attended, wo[...], preferred_element_type=jnp.float32)
+        projected = 0.0
+        for ahead in range(groups):
+            group = lax.rem(mine + ahead, groups)
+            if ahead > 0:
+                for head in range(heads):
+                    att_arrived(step, slot, head, ahead)
+            attended = jnp.concatenate([att[step, slot, group, head] for head in range(heads)], axis=1)
+            rows_here = pl.ds(pl.multiple_of(group * block, 128), block)
+            projected += jnp.dot(attended, wo[rows_here, :], preferred_element_type=jnp.float32)
         layer_out = (residual + gate_row * projected).astype(jnp.bfloat16)
         ends = (pipe == last) & (step == steps - 1)
 
@@ -280,9 +294,15 @@
                 @pl.when(jnp.logical_not(own))
                 def _():
                     remote(source, fin.at[slot], send, fin_recv.at[slot], to_pipe, to_seq).start()
+
+    def visit(step, carry):
+        for slot in range(micro):
+            first_half(step, slot)
+        for slot in range(micro):
+            second_half(step, slot)
         return carry
 
-    lax.fori_loop(0, micro * steps, visit, 0)
+    lax.fori_loop(0, steps, visit, 0)
 
     for slot in range(micro):
         pltpu.make_async_copy(fin_src.at[slot, 0, pl.ds(0, rows), :], fin.at[slot],
@@ -312,8 +332,9 @@
     def drain(item, carry):
         step, slot = item // micro, item % micro
         ends = (pipe == last) & (step == steps - 1)
-        for ahead in range(1, groups):
-            att_copy(step, slot, ahead).wait_send()
+        for head in range(heads):
+            for ahead in range(1, groups):
+                att_copy(step, slot, head, ahead).wait_send()
 
         @pl.when(jnp.logical_not((pipe == 0) & (step == 0)))
         def _():
@@ -359,28 +380,31 @@
     per_block, per_part = n_pipe // groups, n_seq // sharers
     bf16, f32 = jnp.bfloat16, jnp.float32
     vmem = pl.BlockSpec(memory_space=pltpu.VMEM)
-    smem = pl.BlockSpec(memory_space=pltpu.SMEM)
     hbm = pl.BlockSpec(memory_space=pl.ANY)
     dma = pltpu.SemaphoreType.DMA
     return pl.pallas_call(
         functools.partial(kernel, n_pipe, n_seq, groups, micro, steps, head_dim),
         out_shape=jax.ShapeDtypeStruct(latents.shape, bf16),
-        in_specs=[vmem, smem, smem, vmem, vmem, hbm, hbm, hbm],
+        in_specs=[hbm] * 8,
         out_specs=vmem,
         scratch_shapes=[
+            pltpu.SMEM(timesteps.shape, timesteps.dtype),
+            pltpu.SMEM(step_sizes.shape, f32),
+            pltpu.VMEM(mod_table.shape, f32),
+            pltpu.VMEM(qk_gain.shape, f32),
             pltpu.VMEM((width, block), bf16),
             pltpu.VMEM((width, block), bf16),
             pltpu.VMEM((width, block), bf16),
             pltpu.VMEM((inner, block), bf16),
             pltpu.VMEM((n_pipe, n_seq, micro, rows, share), bf16),
             pltpu.VMEM((steps, micro, groups, sharers, part, block), bf16),
-            pltpu.VMEM((steps, micro, groups, part, block), bf16),
+            pltpu.VMEM((steps, micro, groups, block // head_dim, part, head_dim), bf16),
             pltpu.VMEM((steps, micro, part, block), bf16),
             pltpu.VMEM((micro, part, block), f32),
             pltpu.VMEM((rows * n_seq, width), bf16),
             pltpu.VMEM((micro, per_block, part, share), f32),
             pltpu.VMEM((micro, rows, share), f32),
-            dma((2,)),
+            dma((6,)),
             dma((2, n_seq)),
             dma((2, groups)),
             dma((2, groups, sharers)),
@@ -389,13 +413,13 @@
             dma((steps, micro, groups, sharers)),
             dma((steps, micro, groups)),
             dma((steps, micro, groups, sharers)),
-            dma((steps, micro, groups)),
-            dma((steps, micro, groups)),
+            dma((steps, micro, groups, block // head_dim)),
+            dma((steps, micro, block // head_dim, groups)),
             dma((micro, per_block, per_part)),
             dma((micro,)),
         ],
         compiler_params=pltpu.CompilerParams(
-            has_side_effects=True, vmem_limit_bytes=48 * 1024 * 1024
+            has_side_effects=True, vmem_limit_bytes=64 * 1024 * 1024
         ),
         cost_estimate=pl.CostEstimate(
             flops=2 * 4 * rows * n_seq * width * block * micro * steps,

time: 143 us -> 138 us (0.965)
  local copies, waits for them, and re-layouts: 5.55 us -> 1.31 us
    unnamed x13 -> x1, local copies, waits for them, and re-layouts: 5.55 us -> 1.31 us
where the time goes in v2:
time: 138 us
  Pallas kernels  137 us (99%)
    pallas_call x1, Pallas kernels, shards(): pl.pallas_call(functools.partial(kernel, n_pipe, n_seq, groups, micro, st...  137 us

profile of v2, /device:TPU:0, one launch (start us, length us, event | category | flops | bytes accessed | tf_op | source)
XLA Modules:
  0.0 137.8 jit_solution(5324820871795262305)
XLA Ops:
  0.0 136.5 %denoise.1 = bf16[2,8,384]{2,1,0:T(8,128)(2,1)} custom-call(bf16[2,8,384]{2,1,0:T(8,128)(2,1)} %lat_ref.1, s32[2,2]{1,0:T(2,128)} %ts_hbm.1, f32[16]{0:T(128)} %ss_hbm.1, f32[1,16,4608]{2,1,0:T(8,128)} %mod_hbm.1, f32[1,2,128]{2,1,0:T(2,128)} %gain_hbm.1, bf16[1,1536,1536]{2,1,0:T(8,128)(2,1)} %wq_hbm.1, bf16[1,192,3072]{2,1,0:T(8,128)(2,1)} %wkv_hbm.1, ...), custom_call_target="tpu_custom_call" | custom-call | flops 1207959552 | bytes 4718592 | tf_op jit(solution)/shard_map/denoise/pallas_call | solution.py:385
  136.5 1.3 copy.10

commit v3 on v2

--- a/solution.py
+++ b/solution.py
@@ -21,9 +21,10 @@
     n_pipe, n_seq, groups, micro, steps, head_dim,
     lat_ref, ts_hbm, ss_hbm, mod_hbm, gain_hbm, wq_hbm, wkv_hbm, wo_hbm,
     out_ref,
-    ts_ref, ss_ref, mod_ref, gain_ref, wq, wk, wv, wo, latbuf, hid, att, outb, prev, modded, fin_src, fin,
-    local_sem, kv_recv, kv_send, kv_fwd, lat_send, lat_recv,
-    hid_recv, hid_send, hid_fwd, att_recv, att_send, fin_send, fin_recv,
+    ts_ref, ss_ref, mod_ref, gain_ref, wq, wk, wv, wo, wrows, latbuf, hid, att, outb, prev, modded,
+    first_x, first_mod, slabs, pbuf, pin, csum, cin, pre, kvx, fin_src, fin,
+    local_sem, kv_recv, kv_send, kv_fwd, lat_send, lat_recv, pin_send, pin_recv, cin_send, cin_recv,
+    hid_recv, hid_send, kvx_send, kvx_recv, att_recv, att_send, fin_send, fin_recv,
 ):
     sharers = n_seq // groups
     rows, share = lat_ref.shape[1], lat_ref.shape[2]
@@ -109,40 +110,104 @@
     own_columns = pl.ds(pl.multiple_of(mine * block, 128), block)
     copy_q = pltpu.make_async_copy(wq_hbm.at[0, :, own_columns], wq, local_sem.at[0])
     copy_o = pltpu.make_async_copy(wo_hbm.at[0, :, own_columns], wo, local_sem.at[1])
-    for kv in range(2):
-        for ahead in range(groups - 1, 0, -1):
-            kv_copy(kv, ahead).start()
-    for kv in range(2):
-        pltpu.make_async_copy(columns(kv, mine), slab(kv, seq), kv_recv.at[kv, seq]).start()
-        for step in range(1, sharers):
-            kv_pass(kv, 0, step).start()
+    def weights_start():
+        for kv in range(2):
+            for ahead in range(groups - 1, 0, -1):
+                kv_copy(kv, ahead).start()
+        for kv in range(2):
+            pltpu.make_async_copy(columns(kv, mine), slab(kv, seq), kv_recv.at[kv, seq]).start()
+            for step in range(1, sharers):
+                kv_pass(kv, 0, step).start()
+
+    def weights_finish():
+        for kv in range(2):
+            for ahead in range(1, groups):
+                kv_arrived(kv, lax.rem(mine + ahead, groups) * sharers + sharer)
+                for step in range(1, sharers):
+                    kv_pass(kv, ahead, step).start()
+        for kv in range(2):
+            kv_arrived(kv, seq)
+            for step in range(1, sharers):
+                for group in range(groups):
+                    kv_arrived(kv, group * sharers + lax.rem(sharer + step, sharers))
+
+    pl.when(pipe != 0)(weights_start)
     locals_in = [
         copy_q, copy_o,
         pltpu.make_async_copy(ts_hbm, ts_ref, local_sem.at[2]),
         pltpu.make_async_copy(ss_hbm, ss_ref, local_sem.at[3]),
         pltpu.make_async_copy(mod_hbm, mod_ref, local_sem.at[4]),
         pltpu.make_async_copy(gain_hbm, gain_ref, local_sem.at[5]),
+        pltpu.make_async_copy(wkv_hbm.at[0], wrows, local_sem.at[6]),
     ]
     for copy in locals_in:
         copy.start()
-    for kv in range(2):
-        for ahead in range(1, groups):
-            kv_arrived(kv, lax.rem(mine + ahead, groups) * sharers + sharer)
-            for step in range(1, sharers):
-                kv_pass(kv, ahead, step).start()
-    for kv in range(2):
-        kv_arrived(kv, seq)
-        for step in range(1, sharers):
-            for group in range(groups):
-                kv_arrived(kv, group * sharers + lax.rem(sharer + step, sharers))
     for copy in locals_in:
         copy.wait()
+
+    def modulate(as_float, tau):
+        center = jnp.mean(as_float, axis=-1, keepdims=True)
+        away = as_float - center
+        spread = jnp.mean(away * away, axis=-1, keepdims=True)
+        shift_row = mod_ref[0, pl.ds(tau, 1), 0:width]
+        scale_row = mod_ref[0, pl.ds(tau, 1), width:2 * width]
+        return (
+            away * lax.rsqrt(spread + norm_eps) * (1.0 + scale_row) + shift_row
+        ).astype(jnp.bfloat16)
+
+    def pin_copy(slot, ahead):
+        other = lax.rem(sharer + ahead, sharers)
+        return remote(pbuf.at[slot, other], pin.at[slot, sharer], pin_send.at[slot, ahead],
+                      pin_recv.at[slot, sharer], pipe, mine * sharers + other)
+
+    def cin_copy(slot, ahead):
+        group = lax.rem(mine + ahead, groups)
+        return remote(csum.at[slot, group], cin.at[slot, mine], cin_send.at[slot, ahead],
+                      cin_recv.at[slot, mine], pipe, group * sharers + sharer)
 
     @pl.when(pipe == 0)
     def _():
         for from_pipe in range(n_pipe):
             for from_seq in range(n_seq):
                 lat_arrived(from_pipe, from_seq)
+        for slot in range(micro):
+            pieces = []
+            for from_pipe in range(n_pipe):
+                pieces.append(jnp.concatenate([
+                    latbuf[from_pipe, index, slot].astype(jnp.float32) for index in range(n_seq)
+                ], axis=0))
+            whole = jnp.concatenate(pieces, axis=1)
+            first_x[...] = whole.astype(jnp.bfloat16)
+            mine_rows = pl.ds(pl.multiple_of(sharer * part, 16), part)
+            for group in range(groups):
+                hid[0, slot, group] = first_x[mine_rows, group * block:(group + 1) * block]
+            whole_mod = modulate(whole, ts_ref[0, slot])
+            first_mod[slot] = whole_mod
+            for index in range(n_seq):
+                slabs[index] = whole_mod[:, index * depth:(index + 1) * depth]
+            feature_rows = slabs[seq]
+            for kv in range(2):
+                for group in range(groups):
+                    start = kv * inner + group * block
+                    partial = jnp.dot(feature_rows, wrows[:, start:start + block],
+                                      preferred_element_type=jnp.float32).astype(jnp.bfloat16)
+                    for at in range(sharers):
+                        pbuf[slot, at, group, kv] = partial[at * part:(at + 1) * part]
+            for ahead in range(1, sharers):
+                pin_copy(slot, ahead).start()
+        for slot in range(micro):
+            for ahead in range(1, sharers):
+                other = lax.rem(sharer + ahead, sharers)
+                pltpu.make_async_copy(pbuf.at[slot, other], pin.at[slot, other],
+                                      pin_recv.at[slot, other]).wait()
+            total = pbuf[slot, sharer].astype(jnp.float32)
+            for ahead in range(1, sharers):
+                total += pin[slot, lax.rem(sharer + ahead, sharers)].astype(jnp.float32)
+            csum[slot] = total.astype(jnp.bfloat16)
+            for ahead in range(1, groups):
+                cin_copy(slot, ahead).start()
+
+    pl.when(pipe != 0)(weights_finish)
 
     @pl.when(pipe == last)
     def _():
@@ -159,29 +224,29 @@
     def hid_send_copy(step, slot, group):
         at_last = pipe == last
         to_step = step + jnp.where(at_last, 1, 0)
-        return remote(outb.at[step, slot], hid.at[to_step, slot, mine, sharer],
-                      hid_send.at[step, slot, group], hid_recv.at[to_step, slot, mine, sharer],
+        return remote(outb.at[step, slot], hid.at[to_step, slot, mine],
+                      hid_send.at[step, slot, group], hid_recv.at[to_step, slot, mine],
                       lax.rem(pipe + 1, n_pipe), group * sharers + sharer)
 
-    def hid_pass(step, slot, group, ahead):
-        return remote(hid.at[step, slot, group, sharer], hid.at[step, slot, group, sharer],
-                      hid_fwd.at[step, slot, group, ahead], hid_recv.at[step, slot, group, sharer],
-                      pipe, mine * sharers + lax.rem(sharer + ahead, sharers))
-
-    def hid_arrived(step, slot, group, from_sharer):
-        pltpu.make_async_copy(outb.at[step, slot], hid.at[step, slot, group, from_sharer],
-                              hid_recv.at[step, slot, group, from_sharer]).wait()
-
-    def att_copy(step, slot, head, ahead):
+    def hid_arrived(step, slot, group):
+        pltpu.make_async_copy(outb.at[step, slot], hid.at[step, slot, group],
+                              hid_recv.at[step, slot, group]).wait()
+
+    def kvx_copy(step, slot, ahead):
+        other = lax.rem(sharer + ahead, sharers)
+        return remote(kvx.at[step, slot, sharer], kvx.at[step, slot, sharer], kvx_send.at[step, slot, ahead],
+                      kvx_recv.at[step, slot, sharer], pipe, mine * sharers + other)
+
+    def att_copy(step, slot, ahead):
         group = lax.rem(mine + ahead, groups)
-        return remote(att.at[step, slot, mine, head], att.at[step, slot, mine, head],
-                      att_send.at[step, slot, head, ahead], att_recv.at[step, slot, mine, head],
+        return remote(att.at[step, slot, mine], att.at[step, slot, mine],
+                      att_send.at[step, slot, ahead], att_recv.at[step, slot, mine],
                       pipe, group * sharers + sharer)
 
-    def att_arrived(step, slot, head, ahead):
+    def att_arrived(step, slot, ahead):
         group = lax.rem(mine + ahead, groups)
-        pltpu.make_async_copy(att.at[step, slot, mine, head], att.at[step, slot, group, head],
-                              att_recv.at[step, slot, group, head]).wait()
+        pltpu.make_async_copy(att.at[step, slot, mine], att.at[step, slot, group],
+                              att_recv.at[step, slot, group]).wait()
 
     def fin_targets(slot):
         for wide in range(per_block):
@@ -196,69 +261,65 @@
 
         @pl.when(from_latents)
         def _():
+            modded[...] = first_mod[slot, pl.ds(pl.multiple_of(sharer * part, 16), part), :]
+            total = csum[slot, mine].astype(jnp.float32)
+            for ahead in range(1, groups):
+                group = lax.rem(mine + ahead, groups)
+                pltpu.make_async_copy(csum.at[slot, group], cin.at[slot, group],
+                                      cin_recv.at[slot, group]).wait()
+                total += cin[slot, group].astype(jnp.float32)
+            pre[...] = total
+
+        @pl.when(jnp.logical_not(from_latents))
+        def _():
             for group in range(groups):
-                pieces = []
-                for wide in range(per_block):
-                    pieces.append(jnp.concatenate([
-                        latbuf[group * per_block + wide, index, slot].astype(jnp.float32)
-                        for index in range(n_seq)
-                    ], axis=0))
-                whole = jnp.concatenate(pieces, axis=1) if per_block > 1 else pieces[0]
-                for at in range(sharers):
-                    hid[0, slot, group, at] = whole[at * part:(at + 1) * part].astype(jnp.bfloat16)
-
-        @pl.when(jnp.logical_not(from_latents))
-        def _():
-            for group in range(groups):
-                hid_arrived(step, slot, group, sharer)
-                for ahead in range(1, sharers):
-                    hid_pass(step, slot, group, ahead).start()
-            for group in range(groups):
-                for ahead in range(1, sharers):
-                    hid_arrived(step, slot, group, lax.rem(sharer + ahead, sharers))
-
-        as_float = jnp.concatenate([
-            jnp.concatenate([hid[step, slot, group, at].astype(jnp.float32) for at in range(sharers)], axis=0)
-            for group in range(groups)
-        ], axis=1)
-        center = jnp.mean(as_float, axis=-1, keepdims=True)
-        away = as_float - center
-        spread = jnp.mean(away * away, axis=-1, keepdims=True)
-        shift_row = mod_ref[0, pl.ds(tau, 1), 0:width]
-        scale_row = mod_ref[0, pl.ds(tau, 1), width:2 * width]
-        modded[...] = (
-            away * lax.rsqrt(spread + norm_eps) * (1.0 + scale_row) + shift_row
-        ).astype(jnp.bfloat16)
-        queries = jnp.dot(modded[pl.ds(pl.multiple_of(sharer * part, 16), part), :], wq[...],
-                          preferred_element_type=jnp.float32)
-        keys = jnp.dot(modded[...], wk[...], preferred_element_type=jnp.float32)
-        values = jnp.dot(modded[...], wv[...], preferred_element_type=jnp.float32).astype(jnp.bfloat16)
+                hid_arrived(step, slot, group)
+            modded[...] = modulate(
+                jnp.concatenate([hid[step, slot, group].astype(jnp.float32) for group in range(groups)], axis=1),
+                tau,
+            )
+            for kv in range(2):
+                pre[kv] = jnp.dot(modded[...], wkv[kv][...], preferred_element_type=jnp.float32)
+
         gain_query, gain_key = gain_ref[0, 0:1, :], gain_ref[0, 1:2, :]
-        for head in range(heads):
-            here = slice(head * head_dim, (head + 1) * head_dim)
-            logits = lax.dot_general(
-                rms_rows(queries[:, here], gain_query), rms_rows(keys[:, here], gain_key),
-                (((1,), (1,)), ((), ())), preferred_element_type=jnp.float32,
-            ) * score_scale
-            weights = jnp.exp(logits)
-            total = jnp.sum(weights, axis=-1, keepdims=True)
-            weighted = jnp.dot(weights.astype(jnp.bfloat16), values[:, here],
-                               preferred_element_type=jnp.float32)
-            att[step, slot, mine, head] = (weighted / total).astype(jnp.bfloat16)
-            for ahead in range(1, groups):
-                att_copy(step, slot, head, ahead).start()
+        slices = [slice(head * head_dim, (head + 1) * head_dim) for head in range(heads)]
+        for here in slices:
+            kvx[step, slot, sharer, 0, :, here] = rms_rows(pre[0, :, here], gain_key)
+        kvx[step, slot, sharer, 1] = pre[1].astype(jnp.bfloat16)
+        for ahead in range(1, sharers):
+            kvx_copy(step, slot, ahead).start()
+        projected = jnp.dot(modded[...], wq[...], preferred_element_type=jnp.float32)
+        queries = [rms_rows(projected[:, here], gain_query) for here in slices]
+        totals, weighted = [0.0] * heads, [0.0] * heads
+        for ahead in range(sharers):
+            owner = lax.rem(sharer + ahead, sharers)
+            if ahead > 0:
+                pltpu.make_async_copy(kvx.at[step, slot, sharer], kvx.at[step, slot, owner],
+                                      kvx_recv.at[step, slot, owner]).wait()
+            for head, here in enumerate(slices):
+                logits = lax.dot_general(
+                    queries[head], kvx[step, slot, owner, 0, :, here],
+                    (((1,), (1,)), ((), ())), preferred_element_type=jnp.float32,
+                ) * score_scale
+                weights = jnp.exp(logits)
+                totals[head] += jnp.sum(weights, axis=-1, keepdims=True)
+                weighted[head] += jnp.dot(weights.astype(jnp.bfloat16), kvx[step, slot, owner, 1, :, here],
+                                          preferred_element_type=jnp.float32)
+        for head, here in enumerate(slices):
+            att[step, slot, mine, :, here] = (weighted[head] / totals[head]).astype(jnp.bfloat16)
+        for ahead in range(1, groups):
+            att_copy(step, slot, ahead).start()
 
     def second_half(step, slot):
         tau = ts_ref[step, slot]
         gate_row = mod_ref[0, pl.ds(tau, 1), pl.ds(pl.multiple_of(2 * width + mine * block, 128), block)]
-        residual = hid[step, slot, mine, sharer].astype(jnp.float32)
+        residual = hid[step, slot, mine].astype(jnp.float32)
         projected = 0.0
         for ahead in range(groups):
             group = lax.rem(mine + ahead, groups)
             if ahead > 0:
-                for head in range(heads):
-                    att_arrived(step, slot, head, ahead)
-            attended = jnp.concatenate([att[step, slot, group, head] for head in range(heads)], axis=1)
+                att_arrived(step, slot, ahead)
+            attended = att[step, slot, group]
             rows_here = pl.ds(pl.multiple_of(group * block, 128), block)
             projected += jnp.dot(attended, wo[rows_here, :], preferred_element_type=jnp.float32)
         layer_out = (residual + gate_row * projected).astype(jnp.bfloat16)
@@ -296,6 +357,11 @@
                     remote(source, fin.at[slot], send, fin_recv.at[slot], to_pipe, to_seq).start()
 
     def visit(step, carry):
+        @pl.when((pipe == 0) & (step == 1))
+        def _():
+            weights_start()
+            weights_finish()
+
         for slot in range(micro):
             first_half(step, slot)
         for slot in range(micro):
@@ -322,6 +388,14 @@
     def _():
         lat_copy(last, keeper, n_seq).wait_send()
 
+    @pl.when(pipe == 0)
+    def _():
+        for slot in range(micro):
+            for ahead in range(1, sharers):
+                pin_copy(slot, ahead).wait_send()
+            for ahead in range(1, groups):
+                cin_copy(slot, ahead).wait_send()
+
     for kv in range(2):
         for ahead in range(1, groups):
             kv_copy(kv, ahead).wait_send()
@@ -332,15 +406,10 @@
     def drain(item, carry):
         step, slot = item // micro, item % micro
         ends = (pipe == last) & (step == steps - 1)
-        for head in range(heads):
-            for ahead in range(1, groups):
-                att_copy(step, slot, head, ahead).wait_send()
-
-        @pl.when(jnp.logical_not((pipe == 0) & (step == 0)))
-        def _():
-            for group in range(groups):
-                for ahead in range(1, sharers):
-                    hid_pass(step, slot, group, ahead).wait_send()
+        for ahead in range(1, groups):
+            att_copy(step, slot, ahead).wait_send()
+        for ahead in range(1, sharers):
+            kvx_copy(step, slot, ahead).wait_send()
 
         @pl.when(jnp.logical_not(ends))
         def _():
@@ -396,25 +465,40 @@
             pltpu.VMEM((width, block), bf16),
             pltpu.VMEM((width, block), bf16),
             pltpu.VMEM((inner, block), bf16),
+            pltpu.VMEM(w_kv.shape[1:], bf16),
             pltpu.VMEM((n_pipe, n_seq, micro, rows, share), bf16),
-            pltpu.VMEM((steps, micro, groups, sharers, part, block), bf16),
-            pltpu.VMEM((steps, micro, groups, block // head_dim, part, head_dim), bf16),
+            pltpu.VMEM((steps, micro, groups, part, block), bf16),
+            pltpu.VMEM((steps, micro, groups, part, block), bf16),
             pltpu.VMEM((steps, micro, part, block), bf16),
             pltpu.VMEM((micro, part, block), f32),
+            pltpu.VMEM((part, width), bf16),
             pltpu.VMEM((rows * n_seq, width), bf16),
+            pltpu.VMEM((micro, rows * n_seq, width), bf16),
+            pltpu.VMEM((n_seq, rows * n_seq, w_kv.shape[1]), bf16),
+            pltpu.VMEM((micro, sharers, groups, 2, part, block), bf16),
+            pltpu.VMEM((micro, sharers, groups, 2, part, block), bf16),
+            pltpu.VMEM((micro, groups, 2, part, block), bf16),
+            pltpu.VMEM((micro, groups, 2, part, block), bf16),
+            pltpu.VMEM((2, part, block), f32),
+            pltpu.VMEM((steps, micro, sharers, 2, part, block), bf16),
             pltpu.VMEM((micro, per_block, part, share), f32),
             pltpu.VMEM((micro, rows, share), f32),
-            dma((6,)),
+            dma((7,)),
             dma((2, n_seq)),
             dma((2, groups)),
             dma((2, groups, sharers)),
             dma((n_seq + 1,)),
             dma((n_pipe, n_seq)),
-            dma((steps, micro, groups, sharers)),
+            dma((micro, sharers)),
+            dma((micro, sharers)),
+            dma((micro, groups)),
+            dma((micro, groups)),
             dma((steps, micro, groups)),
-            dma((steps, micro, groups, sharers)),
-            dma((steps, micro, groups, block // head_dim)),
-            dma((steps, micro, block // head_dim, groups)),
+            dma((steps, micro, groups)),
+            dma((steps, micro, sharers)),
+            dma((steps, micro, sharers)),
+            dma((steps, micro, groups)),
+            dma((steps, micro, groups)),
             dma((micro, per_block, per_part)),
             dma((micro,)),
         ],

time: 138 us -> 136 us (0.986)
  Pallas kernels: 137 us -> 135 us
    pallas_call x1, Pallas kernels: 137 us -> 135 us  [shards(): pl.pallas_call(functools.partial(kernel, n_pipe, n_seq, groups, micro, st...]
where the time goes in v3:
time: 136 us
  Pallas kernels  135 us (99%)
    pallas_call x1, Pallas kernels, shards(): pl.pallas_call(functools.partial(kernel, n_pipe, n_seq, groups, micro, st...  135 us

profile of v3, /device:TPU:0, one launch (start us, length us, event | category | flops | bytes accessed | tf_op | source)
XLA Modules:
  0.0 135.9 jit_solution(945179164927701986)
XLA Ops:
  0.0 134.6 %denoise.1 = bf16[2,8,384]{2,1,0:T(8,128)(2,1)} custom-call(bf16[2,8,384]{2,1,0:T(8,128)(2,1)} %lat_ref.1, s32[2,2]{1,0:T(2,128)} %ts_hbm.1, f32[16]{0:T(128)} %ss_hbm.1, f32[1,16,4608]{2,1,0:T(8,128)} %mod_hbm.1, f32[1,2,128]{2,1,0:T(2,128)} %gain_hbm.1, bf16[1,1536,1536]{2,1,0:T(8,128)(2,1)} %wq_hbm.1, bf16[1,192,3072]{2,1,0:T(8,128)(2,1)} %wkv_hbm.1, ...), custom_call_target="tpu_custom_call" | custom-call | flops 1207959552 | bytes 4718592 | tf_op jit(solution)/shard_map/denoise/pallas_call | solution.py:454
  134.6 1.3 copy.10

commit v4 on v3

--- a/solution.py
+++ b/solution.py
@@ -87,7 +87,7 @@
 
     def columns(kv, group):
         start = pl.multiple_of(kv * inner + group * block, 128)
-        return wkv_hbm.at[0, :, pl.ds(start, block)]
+        return wrows.at[:, pl.ds(start, block)]
 
     def slab(kv, owner):
         return wkv[kv].at[pl.ds(pl.multiple_of(owner * depth, 16), depth), :]
@@ -107,6 +107,8 @@
     def kv_arrived(kv, owner):
         pltpu.make_async_copy(columns(kv, mine), slab(kv, owner), kv_recv.at[kv, owner]).wait()
 
+    rows_in = pltpu.make_async_copy(wkv_hbm.at[0], wrows, local_sem.at[6])
+    rows_in.start()
     own_columns = pl.ds(pl.multiple_of(mine * block, 128), block)
     copy_q = pltpu.make_async_copy(wq_hbm.at[0, :, own_columns], wq, local_sem.at[0])
     copy_o = pltpu.make_async_copy(wo_hbm.at[0, :, own_columns], wo, local_sem.at[1])
@@ -131,6 +133,7 @@
                 for group in range(groups):
                     kv_arrived(kv, group * sharers + lax.rem(sharer + step, sharers))
 
+    rows_in.wait()
     pl.when(pipe != 0)(weights_start)
     locals_in = [
         copy_q, copy_o,
@@ -138,7 +141,6 @@
         pltpu.make_async_copy(ss_hbm, ss_ref, local_sem.at[3]),
         pltpu.make_async_copy(mod_hbm, mod_ref, local_sem.at[4]),
         pltpu.make_async_copy(gain_hbm, gain_ref, local_sem.at[5]),
-        pltpu.make_async_copy(wkv_hbm.at[0], wrows, local_sem.at[6]),
     ]
     for copy in locals_in:
         copy.start()

time: 136 us -> 136 us (level)
  no operation moved by 1% of the time
where the time goes in v4:
time: 136 us
  Pallas kernels  135 us (99%)
    pallas_call x1, Pallas kernels, shards(): pl.pallas_call(functools.partial(kernel, n_pipe, n_seq, groups, micro, st...  135 us

profile of v4, /device:TPU:0, one launch (start us, length us, event | category | flops | bytes accessed | tf_op | source)
XLA Modules:
  0.0 135.9 jit_solution(11606970904863564216)
XLA Ops:
  0.0 134.6 %denoise.1 = bf16[2,8,384]{2,1,0:T(8,128)(2,1)} custom-call(bf16[2,8,384]{2,1,0:T(8,128)(2,1)} %lat_ref.1, s32[2,2]{1,0:T(2,128)} %ts_hbm.1, f32[16]{0:T(128)} %ss_hbm.1, f32[1,16,4608]{2,1,0:T(8,128)} %mod_hbm.1, f32[1,2,128]{2,1,0:T(2,128)} %gain_hbm.1, bf16[1,1536,1536]{2,1,0:T(8,128)(2,1)} %wq_hbm.1, bf16[1,192,3072]{2,1,0:T(8,128)(2,1)} %wkv_hbm.1, ...), custom_call_target="tpu_custom_call" | custom-call | flops 1207959552 | bytes 4718592 | tf_op jit(solution)/shard_map/denoise/pallas_call | solution.py:456
  134.6 1.3 copy.10

commit v5 on v4

--- a/solution.py
+++ b/solution.py
@@ -21,7 +21,7 @@
     n_pipe, n_seq, groups, micro, steps, head_dim,
     lat_ref, ts_hbm, ss_hbm, mod_hbm, gain_hbm, wq_hbm, wkv_hbm, wo_hbm,
     out_ref,
-    ts_ref, ss_ref, mod_ref, gain_ref, wq, wk, wv, wo, wrows, latbuf, hid, att, outb, prev, modded,
+    ts_ref, ss_ref, mod_ref, gain_ref, wq, wkv, wo, wrows, latbuf, hid, att, outb, prev, modded,
     first_x, first_mod, slabs, pbuf, pin, csum, cin, pre, kvx, fin_src, fin,
     local_sem, kv_recv, kv_send, kv_fwd, lat_send, lat_recv, pin_send, pin_recv, cin_send, cin_recv,
     hid_recv, hid_send, kvx_send, kvx_recv, att_recv, att_send, fin_send, fin_recv,
@@ -83,14 +83,13 @@
     def _():
         lat_copy(last, keeper, n_seq).start()
 
-    wkv = (wk, wv)
 
     def columns(kv, group):
         start = pl.multiple_of(kv * inner + group * block, 128)
         return wrows.at[:, pl.ds(start, block)]
 
     def slab(kv, owner):
-        return wkv[kv].at[pl.ds(pl.multiple_of(owner * depth, 16), depth), :]
+        return wkv.at[pl.ds(pl.multiple_of(owner * depth, 16), depth), kv * block:(kv + 1) * block]
 
     def kv_copy(kv, ahead):
         group = lax.rem(mine + ahead, groups)
@@ -270,7 +269,8 @@
                 pltpu.make_async_copy(csum.at[slot, group], cin.at[slot, group],
                                       cin_recv.at[slot, group]).wait()
                 total += cin[slot, group].astype(jnp.float32)
-            pre[...] = total
+            pre[:, :block] = total[0]
+            pre[:, block:] = total[1]
 
         @pl.when(jnp.logical_not(from_latents))
         def _():
@@ -280,14 +280,13 @@
                 jnp.concatenate([hid[step, slot, group].astype(jnp.float32) for group in range(groups)], axis=1),
                 tau,
             )
-            for kv in range(2):
-                pre[kv] = jnp.dot(modded[...], wkv[kv][...], preferred_element_type=jnp.float32)
+            pre[...] = jnp.dot(modded[...], wkv[...], preferred_element_type=jnp.float32)
 
         gain_query, gain_key = gain_ref[0, 0:1, :], gain_ref[0, 1:2, :]
         slices = [slice(head * head_dim, (head + 1) * head_dim) for head in range(heads)]
         for here in slices:
-            kvx[step, slot, sharer, 0, :, here] = rms_rows(pre[0, :, here], gain_key)
-        kvx[step, slot, sharer, 1] = pre[1].astype(jnp.bfloat16)
+            kvx[step, slot, sharer, 0, :, here] = rms_rows(pre[:, here], gain_key)
+        kvx[step, slot, sharer, 1] = pre[:, block:].astype(jnp.bfloat16)
         for ahead in range(1, sharers):
             kvx_copy(step, slot, ahead).start()
         projected = jnp.dot(modded[...], wq[...], preferred_element_type=jnp.float32)
@@ -366,7 +365,6 @@
 
         for slot in range(micro):
             first_half(step, slot)
-        for slot in range(micro):
             second_half(step, slot)
         return carry
 
@@ -464,8 +462,7 @@
             pltpu.VMEM(mod_table.shape, f32),
             pltpu.VMEM(qk_gain.shape, f32),
             pltpu.VMEM((width, block), bf16),
-            pltpu.VMEM((width, block), bf16),
-            pltpu.VMEM((width, block), bf16),
+            pltpu.VMEM((width, 2 * block), bf16),
             pltpu.VMEM((inner, block), bf16),
             pltpu.VMEM(w_kv.shape[1:], bf16),
             pltpu.VMEM((n_pipe, n_seq, micro, rows, share), bf16),
@@ -481,7 +478,7 @@
             pltpu.VMEM((micro, sharers, groups, 2, part, block), bf16),
             pltpu.VMEM((micro, groups, 2, part, block), bf16),
             pltpu.VMEM((micro, groups, 2, part, block), bf16),
-            pltpu.VMEM((2, part, block), f32),
+            pltpu.VMEM((part, 2 * block), f32),
             pltpu.VMEM((steps, micro, sharers, 2, part, block), bf16),
             pltpu.VMEM((micro, per_block, part, share), f32),
             pltpu.VMEM((micro, rows, share), f32),

time: 136 us -> 136 us (level)
  no operation moved by 1% of the time
where the time goes in v5:
time: 136 us
  Pallas kernels  134 us (99%)
    pallas_call x1, Pallas kernels, shards(): pl.pallas_call(functools.partial(kernel, n_pipe, n_seq, groups, micro, st...  134 us

profile of v5, /device:TPU:0, one launch (start us, length us, event | category | flops | bytes accessed | tf_op | source)
XLA Modules:
  0.0 135.7 jit_solution(6763893094054960801)
XLA Ops:
  0.0 134.4 %denoise.1 = bf16[2,8,384]{2,1,0:T(8,128)(2,1)} custom-call(bf16[2,8,384]{2,1,0:T(8,128)(2,1)} %lat_ref.1, s32[2,2]{1,0:T(2,128)} %ts_hbm.1, f32[16]{0:T(128)} %ss_hbm.1, f32[1,16,4608]{2,1,0:T(8,128)} %mod_hbm.1, f32[1,2,128]{2,1,0:T(2,128)} %gain_hbm.1, bf16[1,1536,1536]{2,1,0:T(8,128)(2,1)} %wq_hbm.1, bf16[1,192,3072]{2,1,0:T(8,128)(2,1)} %wkv_hbm.1, ...), custom_call_target="tpu_custom_call" | custom-call | flops 1207959552 | bytes 4718592 | tf_op jit(solution)/shard_map/denoise/pallas_call | solution.py:454
  134.4 1.3 copy.10

commit v6 on v5

--- a/solution.py
+++ b/solution.py
@@ -21,9 +21,9 @@
     n_pipe, n_seq, groups, micro, steps, head_dim,
     lat_ref, ts_hbm, ss_hbm, mod_hbm, gain_hbm, wq_hbm, wkv_hbm, wo_hbm,
     out_ref,
-    ts_ref, ss_ref, mod_ref, gain_ref, wq, wkv, wo, wrows, latbuf, hid, att, outb, prev, modded,
+    ts_ref, ss_ref, mod_ref, gain_ref, wq, wkv, wo, stage, latbuf, hid, att, outb, prev, modded,
     first_x, first_mod, slabs, pbuf, pin, csum, cin, pre, kvx, fin_src, fin,
-    local_sem, kv_recv, kv_send, kv_fwd, lat_send, lat_recv, pin_send, pin_recv, cin_send, cin_recv,
+    local_sem, stage_sem, kv_recv, kv_send, kv_fwd, lat_send, lat_recv, pin_send, pin_recv, cin_send, cin_recv,
     hid_recv, hid_send, kvx_send, kvx_recv, att_recv, att_send, fin_send, fin_recv,
 ):
     sharers = n_seq // groups
@@ -84,55 +84,54 @@
         lat_copy(last, keeper, n_seq).start()
 
 
-    def columns(kv, group):
-        start = pl.multiple_of(kv * inner + group * block, 128)
-        return wrows.at[:, pl.ds(start, block)]
-
-    def slab(kv, owner):
-        return wkv.at[pl.ds(pl.multiple_of(owner * depth, 16), depth), kv * block:(kv + 1) * block]
-
-    def kv_copy(kv, ahead):
+    def slab(owner):
+        return wkv.at[pl.ds(pl.multiple_of(owner * depth, 16), depth), :]
+
+    def kv_copy(ahead):
         group = lax.rem(mine + ahead, groups)
-        return remote(columns(kv, group), slab(kv, seq), kv_send.at[kv, ahead],
-                      kv_recv.at[kv, seq], pipe, group * sharers + sharer)
-
-    def kv_pass(kv, ahead, step):
-        group = lax.rem(mine + ahead, groups)
-        owner = group * sharers + sharer
-        source = columns(kv, mine) if ahead == 0 else slab(kv, owner)
-        return remote(source, slab(kv, owner), kv_fwd.at[kv, ahead, step],
-                      kv_recv.at[kv, owner], pipe, mine * sharers + lax.rem(sharer + step, sharers))
-
-    def kv_arrived(kv, owner):
-        pltpu.make_async_copy(columns(kv, mine), slab(kv, owner), kv_recv.at[kv, owner]).wait()
-
-    rows_in = pltpu.make_async_copy(wkv_hbm.at[0], wrows, local_sem.at[6])
-    rows_in.start()
+        return remote(stage.at[group], slab(seq), kv_send.at[ahead],
+                      kv_recv.at[seq], pipe, group * sharers + sharer)
+
+    def kv_pass(ahead, step):
+        owner = lax.rem(mine + ahead, groups) * sharers + sharer
+        source = stage.at[mine] if ahead == 0 else slab(owner)
+        return remote(source, slab(owner), kv_fwd.at[ahead, step],
+                      kv_recv.at[owner], pipe, mine * sharers + lax.rem(sharer + step, sharers))
+
+    def kv_arrived(owner):
+        pltpu.make_async_copy(stage.at[mine], slab(owner), kv_recv.at[owner]).wait()
+
+    def weights_start():
+        for ahead in range(groups - 1, 0, -1):
+            kv_copy(ahead).start()
+        pltpu.make_async_copy(stage.at[mine], slab(seq), kv_recv.at[seq]).start()
+        for step in range(1, sharers):
+            kv_pass(0, step).start()
+
+    def weights_finish():
+        for ahead in range(1, groups):
+            kv_arrived(lax.rem(mine + ahead, groups) * sharers + sharer)
+            for step in range(1, sharers):
+                kv_pass(ahead, step).start()
+        kv_arrived(seq)
+        for step in range(1, sharers):
+            for group in range(groups):
+                kv_arrived(group * sharers + lax.rem(sharer + step, sharers))
+
+    staging = [
+        pltpu.make_async_copy(
+            wkv_hbm.at[0, :, kv * inner + group * block:kv * inner + (group + 1) * block],
+            stage.at[group, :, kv * block:(kv + 1) * block], stage_sem.at[kv, group],
+        )
+        for group in range(groups) for kv in range(2)
+    ]
+    for copy in staging:
+        copy.start()
     own_columns = pl.ds(pl.multiple_of(mine * block, 128), block)
     copy_q = pltpu.make_async_copy(wq_hbm.at[0, :, own_columns], wq, local_sem.at[0])
     copy_o = pltpu.make_async_copy(wo_hbm.at[0, :, own_columns], wo, local_sem.at[1])
-    def weights_start():
-        for kv in range(2):
-            for ahead in range(groups - 1, 0, -1):
-                kv_copy(kv, ahead).start()
-        for kv in range(2):
-            pltpu.make_async_copy(columns(kv, mine), slab(kv, seq), kv_recv.at[kv, seq]).start()
-            for step in range(1, sharers):
-                kv_pass(kv, 0, step).start()
-
-    def weights_finish():
-        for kv in range(2):
-            for ahead in range(1, groups):
-                kv_arrived(kv, lax.rem(mine + ahead, groups) * sharers + sharer)
-                for step in range(1, sharers):
-                    kv_pass(kv, ahead, step).start()
-        for kv in range(2):
-            kv_arrived(kv, seq)
-            for step in range(1, sharers):
-                for group in range(groups):
-                    kv_arrived(kv, group * sharers + lax.rem(sharer + step, sharers))
-
-    rows_in.wait()
+    for copy in staging:
+        copy.wait()
     pl.when(pipe != 0)(weights_start)
     locals_in = [
         copy_q, copy_o,
@@ -187,13 +186,13 @@
             for index in range(n_seq):
                 slabs[index] = whole_mod[:, index * depth:(index + 1) * depth]
             feature_rows = slabs[seq]
-            for kv in range(2):
-                for group in range(groups):
-                    start = kv * inner + group * block
-                    partial = jnp.dot(feature_rows, wrows[:, start:start + block],
-                                      preferred_element_type=jnp.float32).astype(jnp.bfloat16)
-                    for at in range(sharers):
-                        pbuf[slot, at, group, kv] = partial[at * part:(at + 1) * part]
+            for group in range(groups):
+                partial = jnp.dot(feature_rows, stage[group],
+                                  preferred_element_type=jnp.float32).astype(jnp.bfloat16)
+                for at in range(sharers):
+                    for kv in range(2):
+                        pbuf[slot, at, group, kv] = partial[at * part:(at + 1) * part,
+                                                            kv * block:(kv + 1) * block]
             for ahead in range(1, sharers):
                 pin_copy(slot, ahead).start()
         for slot in range(micro):
@@ -207,6 +206,7 @@
             csum[slot] = total.astype(jnp.bfloat16)
             for ahead in range(1, groups):
                 cin_copy(slot, ahead).start()
+        weights_start()
 
     pl.when(pipe != 0)(weights_finish)
 
@@ -360,7 +360,6 @@
     def visit(step, carry):
         @pl.when((pipe == 0) & (step == 1))
         def _():
-            weights_start()
             weights_finish()
 
         for slot in range(micro):
@@ -396,12 +395,11 @@
             for ahead in range(1, groups):
                 cin_copy(slot, ahead).wait_send()
 
-    for kv in range(2):
-        for ahead in range(1, groups):
-            kv_copy(kv, ahead).wait_send()
-        for ahead in range(groups):
-            for step in range(1, sharers):
-                kv_pass(kv, ahead, step).wait_send()
+    for ahead in range(1, groups):
+        kv_copy(ahead).wait_send()
+    for ahead in range(groups):
+        for step in range(1, sharers):
+            kv_pass(ahead, step).wait_send()
 
     def drain(item, carry):
         step, slot = item // micro, item % micro
@@ -464,7 +462,7 @@
             pltpu.VMEM((width, block), bf16),
             pltpu.VMEM((width, 2 * block), bf16),
             pltpu.VMEM((inner, block), bf16),
-            pltpu.VMEM(w_kv.shape[1:], bf16),
+            pltpu.VMEM((groups, w_kv.shape[1], 2 * block), bf16),
             pltpu.VMEM((n_pipe, n_seq, micro, rows, share), bf16),
             pltpu.VMEM((steps, micro, groups, part, block), bf16),
             pltpu.VMEM((steps, micro, groups, part, block), bf16),
@@ -482,10 +480,11 @@
             pltpu.VMEM((steps, micro, sharers, 2, part, block), bf16),
             pltpu.VMEM((micro, per_block, part, share), f32),
             pltpu.VMEM((micro, rows, share), f32),
-            dma((7,)),
-            dma((2, n_seq)),
+            dma((6,)),
             dma((2, groups)),
-            dma((2, groups, sharers)),
+            dma((n_seq,)),
+            dma((groups,)),
+            dma((groups, sharers)),
             dma((n_seq + 1,)),
             dma((n_pipe, n_seq)),
             dma((micro, sharers)),

time: 136 us -> 165 us (1.21)
  Pallas kernels: 134 us -> 164 us
    pallas_call x1, Pallas kernels: 134 us -> 164 us  [shards(): pl.pallas_call(functools.partial(kernel, n_pipe, n_seq, groups, micro, st...]
where the time goes in v6:
time: 165 us
  Pallas kernels  164 us (99%)
    pallas_call x1, Pallas kernels, shards(): pl.pallas_call(functools.partial(kernel, n_pipe, n_seq, groups, micro, st...  164 us

profile of v6, /device:TPU:0, one launch (start us, length us, event | category | flops | bytes accessed | tf_op | source)
XLA Modules:
  0.0 164.8 jit_solution(14373486219475625476)
XLA Ops:
  0.0 163.5 %denoise.1 = bf16[2,8,384]{2,1,0:T(8,128)(2,1)} custom-call(bf16[2,8,384]{2,1,0:T(8,128)(2,1)} %lat_ref.1, s32[2,2]{1,0:T(2,128)} %ts_hbm.1, f32[16]{0:T(128)} %ss_hbm.1, f32[1,16,4608]{2,1,0:T(8,128)} %mod_hbm.1, f32[1,2,128]{2,1,0:T(2,128)} %gain_hbm.1, bf16[1,1536,1536]{2,1,0:T(8,128)(2,1)} %wq_hbm.1, bf16[1,192,3072]{2,1,0:T(8,128)(2,1)} %wkv_hbm.1, ...), custom_call_target="tpu_custom_call" | custom-call | flops 1207959552 | bytes 4718592 | tf_op jit(solution)/shard_map/denoise/pallas_call | solution.py:452
  163.5 1.3 copy.10

commit v7 on v6

--- a/solution.py
+++ b/solution.py
@@ -21,9 +21,9 @@
     n_pipe, n_seq, groups, micro, steps, head_dim,
     lat_ref, ts_hbm, ss_hbm, mod_hbm, gain_hbm, wq_hbm, wkv_hbm, wo_hbm,
     out_ref,
-    ts_ref, ss_ref, mod_ref, gain_ref, wq, wkv, wo, stage, latbuf, hid, att, outb, prev, modded,
+    ts_ref, ss_ref, mod_ref, gain_ref, wq, wkv, wo, stage, relay, latbuf, hid, att, outb, prev, modded,
     first_x, first_mod, slabs, pbuf, pin, csum, cin, pre, kvx, fin_src, fin,
-    local_sem, stage_sem, kv_recv, kv_send, kv_fwd, lat_send, lat_recv, pin_send, pin_recv, cin_send, cin_recv,
+    local_sem, stage_sem, kv_recv, kv_send, kv_fwd, relay_send, relay_recv, lat_send, lat_recv, pin_send, pin_recv, cin_send, cin_recv,
     hid_recv, hid_send, kvx_send, kvx_recv, att_recv, att_send, fin_send, fin_recv,
 ):
     sharers = n_seq // groups
@@ -87,32 +87,55 @@
     def slab(owner):
         return wkv.at[pl.ds(pl.multiple_of(owner * depth, 16), depth), :]
 
-    def kv_copy(ahead):
-        group = lax.rem(mine + ahead, groups)
-        return remote(stage.at[group], slab(seq), kv_send.at[ahead],
-                      kv_recv.at[seq], pipe, group * sharers + sharer)
-
-    def kv_pass(ahead, step):
-        owner = lax.rem(mine + ahead, groups) * sharers + sharer
-        source = stage.at[mine] if ahead == 0 else slab(owner)
-        return remote(source, slab(owner), kv_fwd.at[ahead, step],
+    pairs = [(i, j) for i in range(groups) for j in range(groups) if i != j]
+    relayed = {pair: at for at, pair in enumerate(pair for pair in pairs if abs(pair[0] - pair[1]) > 1)}
+
+    def hop(i, j, k):
+        beyond = k + (1 if j > k else -1)
+        owner = i * sharers + sharer
+        source, send = (stage.at[j], kv_send.at[j]) if k == i else (
+            relay.at[relayed[i, j]], relay_send.at[relayed[i, j]])
+        target, recv = (slab(owner), kv_recv.at[owner]) if beyond == j else (
+            relay.at[relayed[i, j]], relay_recv.at[relayed[i, j]])
+        return remote(source, target, send, recv, pipe, beyond * sharers + sharer)
+
+    def passing(k):
+        return sorted((pair for pair in relayed if min(pair) < k < max(pair)), key=lambda pair: abs(pair[0] - k))
+
+    def kv_pass(group, step, source):
+        owner = group * sharers + sharer
+        return remote(source, slab(owner), kv_fwd.at[group, step],
                       kv_recv.at[owner], pipe, mine * sharers + lax.rem(sharer + step, sharers))
 
     def kv_arrived(owner):
         pltpu.make_async_copy(stage.at[mine], slab(owner), kv_recv.at[owner]).wait()
 
     def weights_start():
-        for ahead in range(groups - 1, 0, -1):
-            kv_copy(ahead).start()
+        for k in range(groups):
+            @pl.when(mine == k)
+            def _():
+                for j in sorted(range(groups), key=lambda j: -abs(j - k)):
+                    if j != k:
+                        hop(k, j, k).start()
         pltpu.make_async_copy(stage.at[mine], slab(seq), kv_recv.at[seq]).start()
         for step in range(1, sharers):
-            kv_pass(0, step).start()
+            kv_pass(mine, step, stage.at[mine]).start()
 
     def weights_finish():
-        for ahead in range(1, groups):
-            kv_arrived(lax.rem(mine + ahead, groups) * sharers + sharer)
-            for step in range(1, sharers):
-                kv_pass(ahead, step).start()
+        for k in range(groups):
+            @pl.when(mine == k)
+            def _():
+                events = [(abs(i - k), 0, i, j) for i, j in passing(k)]
+                events += [(abs(i - k), 1, i, k) for i in range(groups) if i != k]
+                for _, kind, i, j in sorted(events):
+                    if kind == 0:
+                        at = relayed[i, j]
+                        pltpu.make_async_copy(stage.at[0], relay.at[at], relay_recv.at[at]).wait()
+                        hop(i, j, k).start()
+                    else:
+                        kv_arrived(i * sharers + sharer)
+                        for step in range(1, sharers):
+                            kv_pass(i, step, slab(i * sharers + sharer)).start()
         kv_arrived(seq)
         for step in range(1, sharers):
             for group in range(groups):
@@ -206,7 +229,6 @@
             csum[slot] = total.astype(jnp.bfloat16)
             for ahead in range(1, groups):
                 cin_copy(slot, ahead).start()
-        weights_start()
 
     pl.when(pipe != 0)(weights_finish)
 
@@ -360,6 +382,7 @@
     def visit(step, carry):
         @pl.when((pipe == 0) & (step == 1))
         def _():
+            weights_start()
             weights_finish()
 
         for slot in range(micro):
@@ -395,11 +418,17 @@
             for ahead in range(1, groups):
                 cin_copy(slot, ahead).wait_send()
 
-    for ahead in range(1, groups):
-        kv_copy(ahead).wait_send()
-    for ahead in range(groups):
+    for k in range(groups):
+        @pl.when(mine == k)
+        def _():
+            for j in range(groups):
+                if j != k:
+                    hop(k, j, k).wait_send()
+            for i, j in passing(k):
+                hop(i, j, k).wait_send()
+    for group in range(groups):
         for step in range(1, sharers):
-            kv_pass(ahead, step).wait_send()
+            kv_pass(group, step, stage.at[group]).wait_send()
 
     def drain(item, carry):
         step, slot = item // micro, item % micro
@@ -463,6 +492,7 @@
             pltpu.VMEM((width, 2 * block), bf16),
             pltpu.VMEM((inner, block), bf16),
             pltpu.VMEM((groups, w_kv.shape[1], 2 * block), bf16),
+            pltpu.VMEM((max(1, (groups - 1) * (groups - 2)), w_kv.shape[1], 2 * block), bf16),
             pltpu.VMEM((n_pipe, n_seq, micro, rows, share), bf16),
             pltpu.VMEM((steps, micro, groups, part, block), bf16),
             pltpu.VMEM((steps, micro, groups, part, block), bf16),
@@ -485,6 +515,8 @@
             dma((n_seq,)),
             dma((groups,)),
             dma((groups, sharers)),
+            dma((max(1, (groups - 1) * (groups - 2)),)),
+            dma((max(1, (groups - 1) * (groups - 2)),)),
             dma((n_seq + 1,)),
             dma((n_pipe, n_seq)),
             dma((micro, sharers)),

time: 165 us -> 139 us (0.84)
  Pallas kernels: 164 us -> 137 us
    pallas_call x1, Pallas kernels: 164 us -> 137 us  [shards(): pl.pallas_call(functools.partial(kernel, n_pipe, n_seq, groups, micro, st...]
where the time goes in v7:
time: 139 us; the launch traced here: 138 us
  Pallas kernels  137 us (99%)
    pallas_call x1, Pallas kernels, shards(): pl.pallas_call(functools.partial(kernel, n_pipe, n_seq, groups, micro, st...  137 us

profile of v7, /device:TPU:0, one launch (start us, length us, event | category | flops | bytes accessed | tf_op | source)
XLA Modules:
  0.0 138.5 jit_solution(9797106683651005114)
XLA Ops:
  0.0 137.1 %denoise.1 = bf16[2,8,384]{2,1,0:T(8,128)(2,1)} custom-call(bf16[2,8,384]{2,1,0:T(8,128)(2,1)} %lat_ref.1, s32[2,2]{1,0:T(2,128)} %ts_hbm.1, f32[16]{0:T(128)} %ss_hbm.1, f32[1,16,4608]{2,1,0:T(8,128)} %mod_hbm.1, f32[1,2,128]{2,1,0:T(2,128)} %gain_hbm.1, bf16[1,1536,1536]{2,1,0:T(8,128)(2,1)} %wq_hbm.1, bf16[1,192,3072]{2,1,0:T(8,128)(2,1)} %wkv_hbm.1, ...), custom_call_target="tpu_custom_call" | custom-call | flops 1207959552 | bytes 4718592 | tf_op jit(solution)/shard_map/denoise/pallas_call | solution.py:481
  137.2 1.3 copy.10

commit v8 on v5

--- a/solution.py
+++ b/solution.py
@@ -22,7 +22,7 @@
     lat_ref, ts_hbm, ss_hbm, mod_hbm, gain_hbm, wq_hbm, wkv_hbm, wo_hbm,
     out_ref,
     ts_ref, ss_ref, mod_ref, gain_ref, wq, wkv, wo, wrows, latbuf, hid, att, outb, prev, modded,
-    first_x, first_mod, slabs, pbuf, pin, csum, cin, pre, kvx, fin_src, fin,
+    first_x, first_mod, slabs, pbuf, pin, csum, cin, pre, qbuf, kvx, fin_src, fin,
     local_sem, kv_recv, kv_send, kv_fwd, lat_send, lat_recv, pin_send, pin_recv, cin_send, cin_recv,
     hid_recv, hid_send, kvx_send, kvx_recv, att_recv, att_send, fin_send, fin_recv,
 ):
@@ -196,7 +196,6 @@
                         pbuf[slot, at, group, kv] = partial[at * part:(at + 1) * part]
             for ahead in range(1, sharers):
                 pin_copy(slot, ahead).start()
-        for slot in range(micro):
             for ahead in range(1, sharers):
                 other = lax.rem(sharer + ahead, sharers)
                 pltpu.make_async_copy(pbuf.at[slot, other], pin.at[slot, other],
@@ -256,7 +255,7 @@
                 source = fin_src.at[slot, wide, pl.ds(index * rows, rows), :]
                 yield to_pipe, to_seq, source, fin_send.at[slot, wide, index]
 
-    def first_half(step, slot):
+    def project(step, slot):
         tau = ts_ref[step, slot]
         from_latents = (pipe == 0) & (step == 0)
 
@@ -290,7 +289,12 @@
         for ahead in range(1, sharers):
             kvx_copy(step, slot, ahead).start()
         projected = jnp.dot(modded[...], wq[...], preferred_element_type=jnp.float32)
-        queries = [rms_rows(projected[:, here], gain_query) for here in slices]
+        for here in slices:
+            qbuf[slot, :, here] = rms_rows(projected[:, here], gain_query)
+
+    def attend(step, slot):
+        slices = [slice(head * head_dim, (head + 1) * head_dim) for head in range(heads)]
+        queries = [qbuf[slot, :, here] for here in slices]
         totals, weighted = [0.0] * heads, [0.0] * heads
         for ahead in range(sharers):
             owner = lax.rem(sharer + ahead, sharers)
@@ -363,9 +367,14 @@
             weights_start()
             weights_finish()
 
+        project(step, 0)
+        attend(step, 0)
         for slot in range(micro):
-            first_half(step, slot)
+            if slot + 1 < micro:
+                project(step, slot + 1)
             second_half(step, slot)
+            if slot + 1 < micro:
+                attend(step, slot + 1)
         return carry
 
     lax.fori_loop(0, steps, visit, 0)
@@ -479,6 +488,7 @@
             pltpu.VMEM((micro, groups, 2, part, block), bf16),
             pltpu.VMEM((micro, groups, 2, part, block), bf16),
             pltpu.VMEM((part, 2 * block), f32),
+            pltpu.VMEM((micro, part, block), bf16),
             pltpu.VMEM((steps, micro, sharers, 2, part, block), bf16),
             pltpu.VMEM((micro, per_block, part, share), f32),
             pltpu.VMEM((micro, rows, share), f32),

time: 136 us -> 142 us (1.044)
  Pallas kernels: 134 us -> 141 us
    pallas_call x1, Pallas kernels: 134 us -> 141 us  [shards(): pl.pallas_call(functools.partial(kernel, n_pipe, n_seq, groups, micro, st...]
where the time goes in v8:
time: 142 us
  Pallas kernels  141 us (99%)
    pallas_call x1, Pallas kernels, shards(): pl.pallas_call(functools.partial(kernel, n_pipe, n_seq, groups, micro, st...  141 us

profile of v8, /device:TPU:0, one launch (start us, length us, event | category | flops | bytes accessed | tf_op | source)
XLA Modules:
  0.0 142.3 jit_solution(10839653457198466430)
XLA Ops:
  0.0 141.0 %denoise.1 = bf16[2,8,384]{2,1,0:T(8,128)(2,1)} custom-call(bf16[2,8,384]{2,1,0:T(8,128)(2,1)} %lat_ref.1, s32[2,2]{1,0:T(2,128)} %ts_hbm.1, f32[16]{0:T(128)} %ss_hbm.1, f32[1,16,4608]{2,1,0:T(8,128)} %mod_hbm.1, f32[1,2,128]{2,1,0:T(2,128)} %gain_hbm.1, bf16[1,1536,1536]{2,1,0:T(8,128)(2,1)} %wq_hbm.1, bf16[1,192,3072]{2,1,0:T(8,128)(2,1)} %wkv_hbm.1, ...), custom_call_target="tpu_custom_call" | custom-call | flops 1207959552 | bytes 4718592 | tf_op jit(solution)/shard_map/denoise/pallas_call | solution.py:463
  141.0 1.3 copy.10

commit v9 on v5

--- a/solution.py
+++ b/solution.py
@@ -111,10 +111,15 @@
     own_columns = pl.ds(pl.multiple_of(mine * block, 128), block)
     copy_q = pltpu.make_async_copy(wq_hbm.at[0, :, own_columns], wq, local_sem.at[0])
     copy_o = pltpu.make_async_copy(wo_hbm.at[0, :, own_columns], wo, local_sem.at[1])
-    def weights_start():
+    def weights_rest():
         for kv in range(2):
-            for ahead in range(groups - 1, 0, -1):
+            for ahead in range(groups - 1, 1, -1):
                 kv_copy(kv, ahead).start()
+
+    def weights_first():
+        for kv in range(2):
+            if groups > 1:
+                kv_copy(kv, 1).start()
         for kv in range(2):
             pltpu.make_async_copy(columns(kv, mine), slab(kv, seq), kv_recv.at[kv, seq]).start()
             for step in range(1, sharers):
@@ -133,7 +138,8 @@
                     kv_arrived(kv, group * sharers + lax.rem(sharer + step, sharers))
 
     rows_in.wait()
-    pl.when(pipe != 0)(weights_start)
+    pl.when(pipe != 0)(weights_rest)
+    weights_first()
     locals_in = [
         copy_q, copy_o,
         pltpu.make_async_copy(ts_hbm, ts_ref, local_sem.at[2]),
@@ -360,7 +366,7 @@
     def visit(step, carry):
         @pl.when((pipe == 0) & (step == 1))
         def _():
-            weights_start()
+            weights_rest()
             weights_finish()
 
         for slot in range(micro):

time: 136 us -> 149 us (1.096)
  Pallas kernels: 134 us -> 147 us
    pallas_call x1, Pallas kernels: 134 us -> 147 us  [shards(): pl.pallas_call(functools.partial(kernel, n_pipe, n_seq, groups, micro, st...]
where the time goes in v9:
time: 149 us
  Pallas kernels  147 us (99%)
    pallas_call x1, Pallas kernels, shards(): pl.pallas_call(functools.partial(kernel, n_pipe, n_seq, groups, micro, st...  147 us

profile of v9, /device:TPU:0, one launch (start us, length us, event | category | flops | bytes accessed | tf_op | source)
XLA Modules:
  0.0 148.6 jit_solution(2274322666706049600)
XLA Ops:
  0.0 147.3 %denoise.1 = bf16[2,8,384]{2,1,0:T(8,128)(2,1)} custom-call(bf16[2,8,384]{2,1,0:T(8,128)(2,1)} %lat_ref.1, s32[2,2]{1,0:T(2,128)} %ts_hbm.1, f32[16]{0:T(128)} %ss_hbm.1, f32[1,16,4608]{2,1,0:T(8,128)} %mod_hbm.1, f32[1,2,128]{2,1,0:T(2,128)} %gain_hbm.1, bf16[1,1536,1536]{2,1,0:T(8,128)(2,1)} %wq_hbm.1, bf16[1,192,3072]{2,1,0:T(8,128)(2,1)} %wkv_hbm.1, ...), custom_call_target="tpu_custom_call" | custom-call | flops 1207959552 | bytes 4718592 | tf_op jit(solution)/shard_map/denoise/pallas_call | solution.py:460
  147.3 1.3 copy.10

commit v10 on v5

--- a/solution.py
+++ b/solution.py
@@ -23,7 +23,7 @@
     out_ref,
     ts_ref, ss_ref, mod_ref, gain_ref, wq, wkv, wo, wrows, latbuf, hid, att, outb, prev, modded,
     first_x, first_mod, slabs, pbuf, pin, csum, cin, pre, kvx, fin_src, fin,
-    local_sem, kv_recv, kv_send, kv_fwd, lat_send, lat_recv, pin_send, pin_recv, cin_send, cin_recv,
+    local_sem, kv_recv, kv_send, kv_fwd, lat_send, lat_recv, lat_fwd, pin_send, pin_recv, cin_send, cin_recv,
     hid_recv, hid_send, kvx_send, kvx_recv, att_recv, att_send, fin_send, fin_recv,
 ):
     sharers = n_seq // groups
@@ -60,9 +60,15 @@
         pltpu.make_async_copy(lat_ref, latbuf.at[from_pipe, from_seq],
                               lat_recv.at[from_pipe, from_seq]).wait()
 
+    def lat_pass(from_pipe, group, step):
+        from_seq = group * sharers + sharer
+        return remote(latbuf.at[from_pipe, from_seq], latbuf.at[from_pipe, from_seq],
+                      lat_fwd.at[from_pipe, group, step], lat_recv.at[from_pipe, from_seq],
+                      pipe, mine * sharers + lax.rem(sharer + step, sharers))
+
     keeper = (pipe // per_block) * sharers + seq // per_part
-    for ahead in range(n_seq):
-        target = lax.rem(seq + ahead, n_seq)
+    for ahead in range(groups):
+        target = lax.rem(mine + ahead, groups) * sharers + sharer
         if ahead == 0:
             @pl.when(pipe == 0)
             def _():
@@ -169,8 +175,14 @@
     @pl.when(pipe == 0)
     def _():
         for from_pipe in range(n_pipe):
-            for from_seq in range(n_seq):
-                lat_arrived(from_pipe, from_seq)
+            for group in range(groups):
+                lat_arrived(from_pipe, group * sharers + sharer)
+                for step in range(1, sharers):
+                    lat_pass(from_pipe, group, step).start()
+        for from_pipe in range(n_pipe):
+            for group in range(groups):
+                for step in range(1, sharers):
+                    lat_arrived(from_pipe, group * sharers + lax.rem(sharer + step, sharers))
         for slot in range(micro):
             pieces = []
             for from_pipe in range(n_pipe):
@@ -375,8 +387,8 @@
                               fin_recv.at[slot]).wait()
         out_ref[slot] = fin[slot].astype(jnp.bfloat16)
 
-    for ahead in range(n_seq):
-        target = lax.rem(seq + ahead, n_seq)
+    for ahead in range(groups):
+        target = lax.rem(mine + ahead, groups) * sharers + sharer
         if ahead == 0:
             @pl.when(pipe != 0)
             def _():
@@ -393,6 +405,11 @@
         for slot in range(micro):
             for ahead in range(1, sharers):
                 pin_copy(slot, ahead).wait_send()
+        for from_pipe in range(n_pipe):
+            for group in range(groups):
+                for step in range(1, sharers):
+                    lat_pass(from_pipe, group, step).wait_send()
+        for slot in range(micro):
             for ahead in range(1, groups):
                 cin_copy(slot, ahead).wait_send()
 
@@ -488,6 +505,7 @@
             dma((2, groups, sharers)),
             dma((n_seq + 1,)),
             dma((n_pipe, n_seq)),
+            dma((n_pipe, groups, sharers)),
             dma((micro, sharers)),
             dma((micro, sharers)),
             dma((micro, groups)),

time: 136 us -> 137 us (level)
  Pallas kernels: 134 us -> 136 us
    pallas_call x1, Pallas kernels: 134 us -> 136 us  [shards(): pl.pallas_call(functools.partial(kernel, n_pipe, n_seq, groups, micro, st...]
where the time goes in v10:
time: 137 us
  Pallas kernels  136 us (99%)
    pallas_call x1, Pallas kernels, shards(): pl.pallas_call(functools.partial(kernel, n_pipe, n_seq, groups, micro, st...  136 us

profile of v10, /device:TPU:0, one launch (start us, length us, event | category | flops | bytes accessed | tf_op | source)
XLA Modules:
  0.0 137.2 jit_solution(7572889439411923727)
XLA Ops:
  0.0 135.9 %denoise.1 = bf16[2,8,384]{2,1,0:T(8,128)(2,1)} custom-call(bf16[2,8,384]{2,1,0:T(8,128)(2,1)} %lat_ref.1, s32[2,2]{1,0:T(2,128)} %ts_hbm.1, f32[16]{0:T(128)} %ss_hbm.1, f32[1,16,4608]{2,1,0:T(8,128)} %mod_hbm.1, f32[1,2,128]{2,1,0:T(2,128)} %gain_hbm.1, bf16[1,1536,1536]{2,1,0:T(8,128)(2,1)} %wq_hbm.1, bf16[1,192,3072]{2,1,0:T(8,128)(2,1)} %wkv_hbm.1, ...), custom_call_target="tpu_custom_call" | custom-call | flops 1207959552 | bytes 4718592 | tf_op jit(solution)/shard_map/denoise/pallas_call | solution.py:471
  135.9 1.3 copy.10
